TPU v7x, 32 devices: a whole 2x2x4 slice. The times are simulated.
32 devices in a mesh: dp: 8 (over z, y), tm: 4 (over x, core).
Axes of the slice: x: 2, y: 2, z: 4, core: 2. Of those that a mesh axis runs over, the one named last changes fastest.
Arguments:
- frames: bfloat16 [8, 3072, 1536], P('dp', 'tm')
- w_qkv: bfloat16 [1536, 2304], P('dp'), may hold values from -0.15625 to 0.15625
- utt_start: int32 [8, 3], P('dp'), may hold values from 0 to 2943, as said below
- stretch_utt: int32 [8, 12], P('dp'), may hold values from 0 to 2, as said below
- left_stretches: int32 [8, 12], P('dp'), may hold values from 0 to 2, as said below
Outputs:
- context: bfloat16 [8, 3072, 768], P('dp', 'tm')
Inputs may be any that keep to these rules, and one draw needn't show every extreme that they name: `stretch_utt`: in each pack nondecreasing along blocks; utterance u covers one or more whole consecutive blocks; every utterance of 0 to 2 occurs, block 0 in utterance 0. `utt_start`: for utterance u with first block b, at least 256 * b and less than 256 * b + 128. `left_stretches`: at most the number of earlier blocks of the same utterance.
All inputs are finite; a program needn't handle non-finite values.
Results may differ from a plain program's by a relative error of at most 0.0045.
The roundings to bfloat16 on the way count: a program that leaves them out, or rounds other values in their place, can miss the bound.
Values may be sent and summed in bfloat16 or wider, within the bound.
No kernel may reach another device: no remote copies, remote signals or barrier semaphores. Data moves between devices by JAX's collectives and lax.ppermute only.
A program may use at most 64 MiB of HBM per device.

v0:
```python
import functools
import math

import jax
import jax.numpy as jnp
from jax import lax
from jax.experimental import pallas as pl
from jax.experimental.pallas import tpu as pltpu
from jax.sharding import PartitionSpec as P

HEAD_DIM = 96
STRETCH = 256
LEFT = 2
LANES = 128
GROUPS = 4
EXP_SCALE = HEAD_DIM**-0.5 * math.log2(math.e)
REACH = LEFT * STRETCH
MIB = 1024 * 1024


def dot(a, b, dims=((1,), (0,))):
    return lax.dot_general(a, b, (dims, ((), ())), preferred_element_type=jnp.float32)


def head_window(head):
    first = head * HEAD_DIM // LANES * LANES
    last = -(-(head + 1) * HEAD_DIM // LANES) * LANES
    return first, last


def start_all(sems, pairs):
    copies = []
    for i, (*source, target) in enumerate(pairs):
        if len(source) == 1:
            copy = pltpu.make_async_copy(source[0], target, sems.at[i])
            copy.start()
        else:
            for n, choice in enumerate(source[0]):
                copy = pltpu.make_async_copy(choice, target, sems.at[i])
                pl.when(source[1] == n)(copy.start)
        copies.append(copy)
    return copies


class Blocks:
    def __init__(self, blocks, n_late, find):
        self.operands = [operand for block in blocks for operand in block]
        self.counts = [len(block) for block in blocks]
        self.rows = [block[0].shape[0] for block in blocks]
        self.n_late = n_late
        self.early_operands = self.operands[: sum(self.counts[:-n_late])]
        self.find = find

    def copies(self, refs, found, members, target, first=0, columns=slice(None)):
        pairs = []
        for i in members:
            at = sum(self.counts[:i])
            choices = [ref.at[:, columns] for ref in refs[at : at + self.counts[i]]]
            row, which = found[i]
            goal = target.at[pl.ds(pl.multiple_of(row - first, self.rows[i]), self.rows[i])]
            pairs.append((choices[0], goal) if len(choices) == 1 else (choices, which, goal))
        return pairs


def early_kernel(blocks, *refs):
    n = len(blocks.early_operands)
    own_ref, partner_ref, own_sum, partner_sum, w_s, own_s, partner_s, sems = refs[n:]
    found, late_first = blocks.find()
    depth = w_s.shape[0]
    first = jnp.where(late_first == 0, own_ref.shape[1] - depth, 0)
    members = range(len(found) - blocks.n_late)
    pairs = blocks.copies(refs, found, members, w_s, first)
    columns = pl.ds(pl.multiple_of(first, LANES), depth)
    pairs.append((own_ref.at[:, columns], own_s))
    pairs.append((partner_ref.at[:, columns], partner_s))
    for copy in start_all(sems, pairs):
        copy.wait()
    width = w_s.shape[1] // 3
    for x_s, out in ((own_s, own_sum), (partner_s, partner_sum)):
        for third in range(3):
            cols = slice(third * width, (third + 1) * width)
            out[:, cols] = dot(x_s[...], w_s[:, cols])


def project_halo(halo_refs, kv_ref, k_ref, v_ref):
    width = k_ref.shape[1]
    for i, frames_ref in enumerate(halo_refs):
        at = slice(i * STRETCH, (i + 1) * STRETCH)
        k_ref[at, :] = dot(frames_ref[...], kv_ref[:, :width]).astype(jnp.bfloat16)
        v_ref[at, :] = dot(frames_ref[...], kv_ref[:, width:]).astype(jnp.bfloat16)


def late_kernel(blocks, start_ref, owner_ref, left_ref, *refs):
    n = len(blocks.operands)
    own_ref, partner_ref = refs[n : n + 2]
    halo_refs = refs[n + 2 : n + 2 + LEFT]
    own_sum, partner_sum, out_ref, q_out, k_out, v_out, kv_out, *scratch = refs[n + 2 + LEFT :]
    w_s, own_s, partner_s, sems = scratch
    depth = w_s.shape[0]
    width = w_s.shape[1] // 3
    rows = own_s.shape[0]
    core = lax.axis_index("tm") % 2
    found, late_first = blocks.find()
    everything = range(len(found))
    pairs = blocks.copies(refs, found, everything[-blocks.n_late :], w_s, late_first)
    columns = pl.ds(pl.multiple_of(late_first, LANES), depth)
    pairs.append((partner_ref.at[:, columns], partner_s))
    pairs.append((own_ref.at[:, columns], own_s))
    n_first = len(pairs)
    pairs += blocks.copies(refs, found, everything, kv_out, 0, slice(width, 3 * width))
    copies = start_all(sems, pairs)
    for copy in copies[:n_first]:
        copy.wait()
    for x_s, acc, place in ((partner_s, partner_sum, 1 - core), (own_s, own_sum, core)):
        row = pl.multiple_of(place * rows, STRETCH)
        for third, (dst, skip) in enumerate(((q_out, 0), (k_out, REACH), (v_out, REACH))):
            cols = slice(third * width, (third + 1) * width)
            value = (acc[:, cols] + dot(x_s[...], w_s[:, cols])).astype(jnp.bfloat16)
            dst[pl.ds(pl.multiple_of(row + skip, STRETCH), rows), :] = value
    for copy in copies[n_first:]:
        copy.wait()

    @pl.when(core == 1)
    def _():
        project_halo(halo_refs, kv_out, k_out, v_out)

    chunks = rows // STRETCH

    def block_of(i):
        return jnp.where(i < chunks, (1 - core) * chunks + i, i - chunks + LEFT)

    count = jnp.where(core == 0, 2 * chunks - LEFT, chunks)
    attend(start_ref, owner_ref, left_ref, q_out, k_out, v_out, 0, count, block_of, out_ref)


def own_kernel(start_ref, owner_ref, left_ref, q_ref, k_ref, v_ref, kv_ref, *refs):
    *halo_refs, done_ref, out_ref, k_s, v_s = refs
    rows, width = out_ref.shape
    core = lax.axis_index("tm") % 2
    own = pl.multiple_of(core * rows + REACH, STRETCH)
    k_s[REACH:, :] = k_ref[pl.ds(own, rows), :]
    v_s[REACH:, :] = v_ref[pl.ds(own, rows), :]

    @pl.when(core == 0)
    def _():
        project_halo(halo_refs, kv_ref, k_s, v_s)

    @pl.when(core == 1)
    def _():
        k_s[:REACH, :] = k_ref[rows : rows + REACH, :]
        v_s[:REACH, :] = v_ref[rows : rows + REACH, :]

    chunks = rows // STRETCH
    base = core * chunks
    count = jnp.where(core == 0, LEFT, chunks)

    def block_of(i):
        return base + i

    attend(start_ref, owner_ref, left_ref, q_ref, k_s, v_s, base, count, block_of, out_ref)

    @pl.when(core == 0)
    def _():
        out_ref[REACH:, :] = done_ref[rows : 2 * rows - REACH, :]


def attend(start_ref, owner_ref, left_ref, q_s, k_s, v_s, k_base, count, block_of, out_ref):
    width = out_ref.shape[1]
    chunks = q_s.shape[0] // STRETCH
    pair = lax.axis_index("tm") // 2
    lane = lax.broadcasted_iota(jnp.int32, (1, width), 1)
    heads = width // HEAD_DIM

    def attend_block(chunk, start, lowest, q_row, k_row, span, out_ref, out_row):
        first_key = (chunk + 1) * STRETCH - span
        key_frame = first_key + lax.broadcasted_iota(jnp.int32, (1, STRETCH), 1)
        bias = jnp.where(key_frame >= lowest, 0.0, -jnp.inf).astype(jnp.float32)
        frame = chunk * STRETCH + lax.broadcasted_iota(jnp.int32, (STRETCH, 1), 0)
        live = frame >= start
        windows = [head_window(head) for head in range(heads)]
        insides = [
            ((lane >= head * HEAD_DIM) & (lane < (head + 1) * HEAD_DIM))[:, first:last]
            for head, (first, last) in enumerate(windows)
        ]
        tiles = [jnp.zeros((STRETCH, LANES), jnp.float32) for _ in range(width // LANES)]

        def score(head):
            first, last = windows[head]
            q = q_s[pl.ds(q_row, STRETCH), first:last]
            q = jnp.where(insides[head], q, jnp.zeros_like(q))
            return dot(q, k_s[pl.ds(k_row, span), first:last], ((1,), (1,)))

        def weigh(scores):
            scores = [scores[:, at : at + STRETCH] for at in range(0, span, STRETCH)]
            scores[0] = scores[0] + bias
            top = functools.reduce(jnp.maximum, scores)
            top = jnp.max(top, axis=-1, keepdims=True)
            expo = [jnp.exp2((part - top) * EXP_SCALE) for part in scores]
            total = jnp.sum(functools.reduce(jnp.add, expo), axis=-1, keepdims=True)
            share = 1.0 / total
            return jnp.concatenate([(part * share).astype(jnp.bfloat16) for part in expo], axis=1)

        def mix(head, probs):
            first, last = windows[head]
            mixed = dot(probs, v_s[pl.ds(k_row, span), first:last])
            for tile in range(first // LANES, last // LANES):
                at = tile * LANES - first
                tiles[tile] = jnp.where(
                    insides[head][:, at : at + LANES], mixed[:, at : at + LANES], tiles[tile]
                )

        scores = score(0)
        probs = None
        for head in range(heads):
            following = score(head + 1) if head + 1 < heads else None
            weighed = weigh(scores)
            if probs is not None:
                mix(head - 1, probs)
            scores, probs = following, weighed
        mix(heads - 1, probs)
        for tile, value in enumerate(tiles):
            value = jnp.where(live, value, 0.0).astype(jnp.bfloat16)
            out_ref[pl.ds(out_row, STRETCH), tile * LANES : (tile + 1) * LANES] = value

    @pl.loop(0, count)
    def _(i):
        block = block_of(i)
        out_row = pl.multiple_of(i * STRETCH, STRETCH)
        q_row = pl.multiple_of(block * STRETCH, STRETCH)
        chunk = pair * chunks + block
        left = left_ref[0, chunk]
        start = start_ref[0, owner_ref[0, chunk]]
        lowest = jnp.maximum((chunk - left) * STRETCH, start)
        for back in range(LEFT + 1):

            @pl.when(left == back)
            def _():
                k_row = pl.multiple_of((block - k_base + LEFT - back) * STRETCH, STRETCH)
                span = (back + 1) * STRETCH
                attend_block(chunk, start, lowest, q_row, k_row, span, out_ref, out_row)


def after(value, *others):
    return lax.optimization_barrier((value, *others))[0]


SMEM_SPEC = pl.BlockSpec(memory_space=pltpu.SMEM)
VMEM_SPEC = pl.BlockSpec(memory_space=pltpu.VMEM)
ANY_SPEC = pl.BlockSpec(memory_space=pl.ANY)


def half_kernel(w_ref, out_ref, sems):
    width = out_ref.shape[1] // 3
    core = lax.axis_index("tm") % 2
    pairs = []
    for third in range(3):
        at = pl.multiple_of((2 * third + core) * width, LANES)
        pairs.append((w_ref.at[:, pl.ds(at, width)], out_ref.at[:, third * width : (third + 1) * width]))
    for copy in start_all(sems, pairs):
        copy.wait()


def take_half(w):
    return pl.pallas_call(
        half_kernel,
        out_shape=jax.ShapeDtypeStruct((w.shape[0], w.shape[1] // 2), w.dtype),
        in_specs=[pl.BlockSpec(memory_space=pltpu.HBM)],
        out_specs=VMEM_SPEC,
        scratch_shapes=[pltpu.SemaphoreType.DMA((3,))],
        compiler_params=pltpu.CompilerParams(vmem_limit_bytes=4 * MIB),
        name="take_half",
    )(w)


def join_kernel(own_ref, other_ref, out_ref, sems):
    rows, width = own_ref.shape
    core = lax.axis_index("tm") % 2
    own_at = pl.multiple_of(core * width, LANES)
    other_at = pl.multiple_of((1 - core) * width, LANES)
    pairs = [
        (own_ref, out_ref.at[:, pl.ds(own_at, width)]),
        (other_ref.at[:rows, :], out_ref.at[:, pl.ds(other_at, width)]),
    ]
    for copy in start_all(sems, pairs):
        copy.wait()


def join(own, other):
    rows, width = own.shape
    return pl.pallas_call(
        join_kernel,
        out_shape=jax.ShapeDtypeStruct((rows, 2 * width), own.dtype),
        in_specs=[ANY_SPEC] * 2,
        out_specs=ANY_SPEC,
        scratch_shapes=[pltpu.SemaphoreType.DMA((2,))],
        compiler_params=pltpu.CompilerParams(vmem_limit_bytes=4 * MIB),
        name="join",
    )(own, other)


def project_early(blocks, inputs, partner):
    rows, depth = inputs.shape
    depth -= depth // GROUPS
    cols = blocks.operands[0].shape[1]
    n_copies = len(blocks.counts) - blocks.n_late + 2
    return pl.pallas_call(
        functools.partial(early_kernel, blocks),
        out_shape=[jax.ShapeDtypeStruct((rows, cols), jnp.float32)] * 2,
        in_specs=[ANY_SPEC] * (len(blocks.early_operands) + 2),
        out_specs=[VMEM_SPEC] * 2,
        scratch_shapes=[
            pltpu.VMEM((depth, cols), jnp.bfloat16),
            pltpu.VMEM((rows, depth), jnp.bfloat16),
            pltpu.VMEM((rows, depth), jnp.bfloat16),
            pltpu.SemaphoreType.DMA((n_copies,)),
        ],
        compiler_params=pltpu.CompilerParams(vmem_limit_bytes=24 * MIB),
        cost_estimate=pl.CostEstimate(flops=0, bytes_accessed=0, transcendentals=0),
        name="project_early",
    )(*blocks.early_operands, inputs, partner)


def tail_kernel(x_ref, *refs):
    *outs, sems = refs
    first = x_ref.shape[0] - len(outs) * STRETCH
    pairs = [
        (x_ref.at[first + i * STRETCH : first + (i + 1) * STRETCH, :], out)
        for i, out in enumerate(outs)
    ]
    for copy in start_all(sems, pairs):
        copy.wait()


def take_tail(x):
    return pl.pallas_call(
        tail_kernel,
        out_shape=[jax.ShapeDtypeStruct((STRETCH, x.shape[1]), x.dtype)] * LEFT,
        in_specs=[ANY_SPEC],
        out_specs=[VMEM_SPEC] * LEFT,
        scratch_shapes=[pltpu.SemaphoreType.DMA((LEFT,))],
        compiler_params=pltpu.CompilerParams(vmem_limit_bytes=4 * MIB),
        name="take_tail",
    )(x)


def project_late_attend(tables, blocks, inputs, partner, halo, sums):
    rows, depth = inputs.shape
    late_depth = depth // GROUPS
    cols = blocks.operands[0].shape[1]
    width = cols // 3
    keys = jax.ShapeDtypeStruct((2 * rows + REACH, width), jnp.bfloat16)
    return pl.pallas_call(
        functools.partial(late_kernel, blocks),
        out_shape=[
            jax.ShapeDtypeStruct((2 * rows - REACH, width), jnp.bfloat16),
            jax.ShapeDtypeStruct((2 * rows, width), jnp.bfloat16),
            keys,
            keys,
            jax.ShapeDtypeStruct((depth, 2 * width), jnp.bfloat16),
        ],
        in_specs=[SMEM_SPEC] * 3 + [ANY_SPEC] * (len(blocks.operands) + 2) + [VMEM_SPEC] * (LEFT + 2),
        out_specs=[VMEM_SPEC] * 5,
        scratch_shapes=[
            pltpu.VMEM((late_depth, cols), jnp.bfloat16),
            pltpu.VMEM((rows, late_depth), jnp.bfloat16),
            pltpu.VMEM((rows, late_depth), jnp.bfloat16),
            pltpu.SemaphoreType.DMA((len(blocks.counts) + blocks.n_late + 2,)),
        ],
        compiler_params=pltpu.CompilerParams(vmem_limit_bytes=24 * MIB),
        name="project_late_attend",
    )(*tables, *blocks.operands, inputs, partner, *halo, *sums)


def attend_own(tables, queries, keys, values, weights, halo, done):
    rows, width = queries.shape
    rows //= 2
    return pl.pallas_call(
        own_kernel,
        out_shape=jax.ShapeDtypeStruct((rows, width), jnp.bfloat16),
        in_specs=[SMEM_SPEC] * 3 + [VMEM_SPEC] * (LEFT + 5),
        out_specs=VMEM_SPEC,
        scratch_shapes=[pltpu.VMEM((rows + REACH, width), jnp.bfloat16)] * 2,
        compiler_params=pltpu.CompilerParams(vmem_limit_bytes=20 * MIB),
        name="attend_own",
    )(*tables, queries, keys, values, weights, *halo, done)


def at_end():
    place = lax.axis_index("dp") // 2
    return jnp.where((place == 0) | (place == 3), 1, 0)


def choose_kernel(between_ref, end_ref, out_ref, sems):
    for copy in start_all(sems, [((between_ref, end_ref), at_end(), out_ref)]):
        copy.wait()


def choose(between, end):
    return pl.pallas_call(
        choose_kernel,
        out_shape=jax.ShapeDtypeStruct(end.shape, end.dtype),
        in_specs=[ANY_SPEC] * 2,
        out_specs=VMEM_SPEC,
        scratch_shapes=[pltpu.SemaphoreType.DMA((1,))],
        compiler_params=pltpu.CompilerParams(vmem_limit_bytes=2 * MIB),
        name="choose",
    )(between, end)


def gather_neighbours(half):
    size = half.shape[0]

    def along(name, block, hops):
        with jax.named_scope(name):
            return lax.ppermute(
                block, "dp", [(2 * a + s, 2 * b + s) for a, b in hops for s in range(2)]
            )

    def across(name, block, places):
        with jax.named_scope(name):
            return lax.ppermute(
                block, "dp", [(2 * a + s, 2 * a + 1 - s) for a in places for s in range(2)]
            )

    line = range(4)
    outward = [(1, 0), (2, 3)]
    between = [(1, 2), (2, 1)]
    near = along("near", half, outward + [(0, 1), (3, 2)])
    mid = along("mid", half, between)
    half_across = across("half_across", half, line)
    mid_far = along("mid_far", near, between)
    near_across = across("near_across", after(near, half_across, mid), line)
    end_mid = along("end_mid", mid, outward)
    end_far = along("end_far", after(mid_far, end_mid), outward)
    second = choose(mid, end_mid)
    second_across = across("second_across", after(second, near_across), line)
    third = choose(mid_far, end_far)
    third_across = across("third_across", after(third, second_across), line)

    def find():
        index = lax.axis_index("dp")
        place, side = index // 2, index % 2
        is_end = at_end()
        second = jnp.where(is_end == 1, place ^ 2, 3 - place)
        third = jnp.where(is_end == 1, 3 - place, place ^ 2)
        spots = (place, place ^ 1, second, third)
        found = [((2 * spot + (side ^ n)) * size, is_end) for spot in spots for n in range(2)]
        return found, third * 2 * size

    blocks = [
        (half,),
        (half_across,),
        (near,),
        (near_across,),
        (second,),
        (second_across,),
        (third,),
        (third_across,),
    ]
    marks = (near_across, mid_far, end_mid), (second_across, end_far), (third_across,)
    return Blocks(blocks, 2, find), marks


def local(frames, w_qkv, utt_start, stretch_utt, left_stretches):
    inputs = frames[0]
    depth = inputs.shape[1]
    members = lax.axis_size("tm")

    half = take_half(w_qkv)

    tail = take_tail(after(inputs, half))
    with jax.named_scope("partner"):
        partner = lax.ppermute(inputs, "tm", [(i, i ^ 1) for i in range(members)])
    if lax.axis_size("dp") == 8:
        blocks, marks = gather_neighbours(half)
    else:
        weights = lax.all_gather(half, "dp", axis=0, tiled=True)
        late_first = depth - depth // GROUPS
        found = [(0, 0), (late_first, 0)], late_first
        parts = [(weights[:late_first],), (weights[late_first:],)]
        blocks, marks = Blocks(parts, 1, lambda: found), ((half,),) * 3

    with jax.named_scope("halo"):
        onward = [(i, i + 2) for i in range(1, members - 2, 2)]
        halo = [lax.ppermute(after(x, *mark), "tm", onward) for x, mark in zip(tail, marks)]

    tables = (utt_start, stretch_utt, left_stretches)
    sums = project_early(blocks, inputs, partner)
    with jax.named_scope("halo_first"):
        back = [(i + 1, i) for i in range(0, members, 2)]
        halo_first = [lax.ppermute(after(x, *sums), "tm", back) for x in halo]
    attended, queries, keys, values, weights = project_late_attend(
        tables, blocks, inputs, partner, halo, sums
    )
    with jax.named_scope("swap"):
        other = lax.ppermute(attended, "tm", [(i, i ^ 1) for i in range(members)])
    own_out = attend_own(tables, queries, keys, values, weights, halo_first, attended)
    return join(own_out, other)[None]


def solution(mesh):
    return jax.shard_map(
        local,
        mesh=mesh,
        in_specs=(P("dp", "tm", None), P("dp", None), P("dp", None), P("dp", None), P("dp", None)),
        out_specs=P("dp", "tm", None),
        check_vma=False,
    )
```

profile of v0, /device:TPU:0, one launch (start us, length us, event | category | flops | bytes accessed | tf_op | source)
XLA Modules:
  0.0 75.1 jit_solution(959260400821175414)
XLA Ops:
  0.0 0.0 copy-start
  0.0 0.5 collective-permute-start.9
  0.5 0.0 copy-start.1
  0.5 1.4 %copy-done.1 = bf16[192,2304]{1,0:T(8,128)(2,1)S(1)} copy-done((bf16[192,2304]{1,0:T(8,128)(2,1)S(1)}, bf16[192,2304]{1,0:T(8,128)(2,1)}, u32[]{:S(2)}) %copy-start.1) | copy-done | bytes 884760
  1.9 0.1 take_half.1.refs_0_
  1.9 2.5 %collective-permute-start = (bf16[192,1152]{1,0:T(8,128)(2,1)S(1)}, bf16[192,1152]{1,0:T(8,128)(2,1)S(1)}, u32[]{:S(2)}, u32[]{:S(2)}) collective-permute-start(bf16[192,1152]{1,0:T(8,128)(2,1)S(1)} %take_half.1.refs_0_), channel_id=1, source_target_pairs={{0,4},{4,0},{8,12},{12,8},{16,20},{20,16},{24,28},{28,24},{1,5},{5... | collective-permute-start | bytes 1327112 | tf_op jit(solution)/shard_map/half_across/ppermute | solution.py:421
  4.5 1.6 %collective-permute-start.1 = (bf16[192,1152]{1,0:T(8,128)(2,1)S(1)}, bf16[192,1152]{1,0:T(8,128)(2,1)S(1)}, u32[]{:S(2)}, u32[]{:S(2)}) collective-permute-start(bf16[192,1152]{1,0:T(8,128)(2,1)S(1)} %take_half.1.refs_0_), channel_id=1, source_target_pairs={{8,0},{12,4},{16,24},{20,28},{0,8},{4,12},{24,16},{28,20},{9,1},{1... | collective-permute-start | bytes 1327112 | tf_op jit(solution)/shard_map/near/ppermute | solution.py:415
  6.1 0.7 collective-permute-start.2
  6.7 8.4 %collective-permute-done.refs_1_ = bf16[192,1152]{1,0:T(8,128)(2,1)S(1)} collective-permute-done((bf16[192,1152]{1,0:T(8,128)(2,1)S(1)}, bf16[192,1152]{1,0:T(8,128)(2,1)S(1)}, u32[]{:S(2)}, u32[]{:S(2)}) %collective-permute-start) | collective-permute-done | bytes 442400 | tf_op jit(solution)/shard_map/half_across/ppermute | solution.py:421
  15.2 1.5 %collective-permute-done.1.refs_2_ = bf16[192,1152]{1,0:T(8,128)(2,1)S(1)} collective-permute-done((bf16[192,1152]{1,0:T(8,128)(2,1)S(1)}, bf16[192,1152]{1,0:T(8,128)(2,1)S(1)}, u32[]{:S(2)}, u32[]{:S(2)}) %collective-permute-start.1) | collective-permute-done | bytes 442400 | tf_op jit(solution)/shard_map/near/ppermute | solution.py:415
  16.6 0.0 collective-permute-done.2.between_ref
  16.6 1.3 %collective-permute-start.4 = (bf16[192,1152]{1,0:T(8,128)(2,1)S(1)}, bf16[192,1152]{1,0:T(8,128)(2,1)S(1)}, u32[]{:S(2)}, u32[]{:S(2)}) collective-permute-start(bf16[192,1152]{1,0:T(8,128)(2,1)S(1)} %collective-permute-done.2.between_ref), channel_id=1, source_target_pairs={{8,0},{12,4},{16,24},{20,28},{9,1},{13,5},{17,25},{21,29},{10,2},{... | collective-permute-start | bytes 1327112 | tf_op jit(solution)/shard_map/end_mid/ppermute | solution.py:415
  17.9 0.4 collective-permute-start.3
  18.3 0.7 collective-permute-start.6
  19.0 13.0 %collective-permute-done.4.end_ref = bf16[192,1152]{1,0:T(8,128)(2,1)S(1)} collective-permute-done((bf16[192,1152]{1,0:T(8,128)(2,1)S(1)}, bf16[192,1152]{1,0:T(8,128)(2,1)S(1)}, u32[]{:S(2)}, u32[]{:S(2)}) %collective-permute-start.4) | collective-permute-done | bytes 442400 | tf_op jit(solution)/shard_map/end_mid/ppermute | solution.py:415
  32.1 0.3 choose.2.refs_4_
  32.3 0.0 collective-permute-done.3.refs_3_
  32.3 0.6 collective-permute-start.5
  32.9 0.0 collective-permute-done.6.between_ref
  32.9 1.3 %collective-permute-start.7 = (bf16[192,1152]{1,0:T(8,128)(2,1)S(1)}, bf16[192,1152]{1,0:T(8,128)(2,1)S(1)}, u32[]{:S(2)}, u32[]{:S(2)}) collective-permute-start(bf16[192,1152]{1,0:T(8,128)(2,1)S(1)} %collective-permute-done.6.between_ref), channel_id=1, source_target_pairs={{8,0},{12,4},{16,24},{20,28},{9,1},{13,5},{17,25},{21,29},{10,2},{... | collective-permute-start | bytes 1327112 | tf_op jit(solution)/shard_map/end_far/ppermute | solution.py:415
  34.2 0.0 copy-done
  34.2 0.1 take_tail.1
  34.4 0.7 collective-permute-start.10
  35.1 8.0 %collective-permute-done.5.refs_5_ = bf16[192,1152]{1,0:T(8,128)(2,1)S(1)} collective-permute-done((bf16[192,1152]{1,0:T(8,128)(2,1)S(1)}, bf16[192,1152]{1,0:T(8,128)(2,1)S(1)}, u32[]{:S(2)}, u32[]{:S(2)}) %collective-permute-start.5) | collective-permute-done | bytes 442400 | tf_op jit(solution)/shard_map/second_across/ppermute | solution.py:421
  43.1 2.6 %collective-permute-done.7.end_ref = bf16[192,1152]{1,0:T(8,128)(2,1)S(1)} collective-permute-done((bf16[192,1152]{1,0:T(8,128)(2,1)S(1)}, bf16[192,1152]{1,0:T(8,128)(2,1)S(1)}, u32[]{:S(2)}, u32[]{:S(2)}) %collective-permute-start.7) | collective-permute-done | bytes 442400 | tf_op jit(solution)/shard_map/end_far/ppermute | solution.py:415
  45.7 0.7 collective-permute-start.11
  46.4 0.3 choose.3.refs_6_
  46.7 0.0 copy-start.2
  46.7 0.0 copy-start.3
  46.7 0.0 copy-start.4
  46.7 1.6 %collective-permute-start.8 = (bf16[192,1152]{1,0:T(8,128)(2,1)S(1)}, bf16[192,1152]{1,0:T(8,128)(2,1)S(1)}, u32[]{:S(2)}, u32[]{:S(2)}) collective-permute-start(bf16[192,1152]{1,0:T(8,128)(2,1)S(1)} %choose.3.refs_6_), channel_id=1, source_target_pairs={{0,4},{4,0},{8,12},{12,8},{16,20},{20,16},{24,28},{28,24},{1,5},{5... | collective-permute-start | bytes 1327112 | tf_op jit(solution)/shard_map/third_across/ppermute | solution.py:421
  48.3 0.0 collective-permute-done.9.refs_7_.refs_9_
  48.3 7.8 %project_early.1 = (f32[768,1152]{1,0:T(8,128)S(1)}, f32[768,1152]{1,0:T(8,128)S(1)}) custom-call(bf16[192,1152]{1,0:T(8,128)(2,1)S(1)} %take_half.1.refs_0_, bf16[192,1152]{1,0:T(8,128)(2,1)S(1)} %collective-permute-done.refs_1_, bf16[192,1152]{1,0:T(8,128)(2,1)S(1)} %collective-permute-done.1.refs_2_, ...), custom_call_target="tpu_custom_call" | custom-call | tf_op jit(solution)/shard_map/project_early/pallas_call | solution.py:306
  56.1 0.0 collective-permute-done.10.refs_10_
  56.1 1.3 %collective-permute-start.12 = (bf16[256,1536]{1,0:T(8,128)(2,1)S(1)}, bf16[256,1536]{1,0:T(8,128)(2,1)S(1)}, u32[]{:S(2)}, u32[]{:S(2)}) collective-permute-start(bf16[256,1536]{1,0:T(8,128)(2,1)S(1)} %collective-permute-done.10.refs_10_), channel_id=1, source_target_pairs={{1,0},{3,2},{5,4},{7,6},{9,8},{11,10},{13,12},{15,14},{17,16},{19,... | collective-permute-start | bytes 2359304 | tf_op jit(solution)/shard_map/halo_first/ppermute | solution.py:491
  57.4 0.0 collective-permute-done.11.refs_11_
  57.4 1.3 %collective-permute-start.13 = (bf16[256,1536]{1,0:T(8,128)(2,1)S(1)}, bf16[256,1536]{1,0:T(8,128)(2,1)S(1)}, u32[]{:S(2)}, u32[]{:S(2)}) collective-permute-start(bf16[256,1536]{1,0:T(8,128)(2,1)S(1)} %collective-permute-done.11.refs_11_), channel_id=1, source_target_pairs={{1,0},{3,2},{5,4},{7,6},{9,8},{11,10},{13,12},{15,14},{17,16},{19,... | collective-permute-start | bytes 2359304 | tf_op jit(solution)/shard_map/halo_first/ppermute | solution.py:491
  58.7 0.0 collective-permute-done.8.refs_7_
  58.8 0.0 copy-done.2
  58.8 0.0 copy-done.3
  58.8 0.0 copy-done.4
  58.8 8.8 %project_late_attend.1 = (bf16[1024,384]{1,0:T(8,128)(2,1)S(1)}, bf16[1536,384]{1,0:T(8,128)(2,1)S(1)}, bf16[2048,384]{1,0:T(8,128)(2,1)S(1)}, bf16[2048,384]{1,0:T(8,128)(2,1)S(1)}, bf16[1536,768]{1,0:T(8,128)(2,1)S(1)}) custom-call(s32[1,3]{1,0:T(1,128)S(1)} %copy-done.2, s32[1,12]{1,0:T(1,128)S(1)} %copy-done.3, s32[1,12]{1,0:T(1,128)S(1)} %copy-done.4, ...), custom_call_target="tpu_custom_call" | custom-call | tf_op jit(solution)/shard_map/project_late_attend/pallas_call | solution.py:352
  67.6 1.9 %collective-permute-start.14 = (bf16[1024,384]{1,0:T(8,128)(2,1)S(1)}, bf16[1024,384]{1,0:T(8,128)(2,1)S(1)}, u32[]{:S(2)}, u32[]{:S(2)}) collective-permute-start(bf16[1024,384]{1,0:T(8,128)(2,1)S(1)} %get-tuple-element.40.refs_2_), channel_id=1, source_target_pairs={{0,1},{1,0},{2,3},{3,2},{4,5},{5,4},{6,7},{7,6},{8,9},{9,8},{10,11... | collective-permute-start | bytes 2359304 | tf_op jit(solution)/shard_map/swap/ppermute | solution.py:496
  69.5 0.0 collective-permute-done.12.refs_0_
  69.5 0.0 collective-permute-done.13.refs_1_
  69.5 4.4 %attend_own.1.own_ref = bf16[768,384]{1,0:T(8,128)(2,1)S(1)} custom-call(s32[1,3]{1,0:T(1,128)S(1)} %copy-done.2, s32[1,12]{1,0:T(1,128)S(1)} %copy-done.3, s32[1,12]{1,0:T(1,128)S(1)} %copy-done.4, bf16[1536,384]{1,0:T(8,128)(2,1)S(1)} %get-tuple-element.34.q_ref, bf16[2048,384]{1,0:T(8,128)(2,1)S(1)} %get-tuple-element.35.k_ref, ...), custom_call_target="tpu_custom_call" | custom-call | tf_op jit(solution)/shard_map/attend_own/pallas_call | solution.py:377
  73.9 0.0 collective-permute-done.14.other_ref
  73.9 1.0 %join.1 = bf16[768,768]{1,0:T(8,128)(2,1)} custom-call(bf16[768,384]{1,0:T(8,128)(2,1)S(1)} %attend_own.1.own_ref, bf16[1024,384]{1,0:T(8,128)(2,1)S(1)} %collective-permute-done.14.other_ref), custom_call_target="tpu_custom_call" | custom-call | tf_op jit(solution)/shard_map/join/pallas_call | solution.py:290
Async XLA Ops:
  0.0 34.2 %copy-start = (bf16[1,768,1536]{2,1,0:T(8,128)(2,1)S(1)}, bf16[1,768,1536]{2,1,0:T(8,128)(2,1)}, u32[]{:S(2)}) copy-start(bf16[1,768,1536]{2,1,0:T(8,128)(2,1)} %param.5) | copy-start | bytes 7077892
  0.0 48.3 %collective-permute-start.9 = (bf16[768,1536]{1,0:T(8,128)(2,1)}, bf16[768,1536]{1,0:T(8,128)(2,1)S(1)}, u32[]{:S(2)}, u32[]{:S(2)}) collective-permute-start(bf16[768,1536]{1,0:T(8,128)(2,1)} %bitcast.2), channel_id=1, source_target_pairs={{0,1},{1,0},{2,3},{3,2},{4,5},{5,4},{6,7},{7,6},{8,9},{9,8},{10,11... | collective-permute-start | bytes 7077896 | tf_op jit(solution)/shard_map/partner/ppermute | solution.py:473
  0.5 1.4 %copy-start.1 = (bf16[192,2304]{1,0:T(8,128)(2,1)S(1)}, bf16[192,2304]{1,0:T(8,128)(2,1)}, u32[]{:S(2)}) copy-start(bf16[192,2304]{1,0:T(8,128)(2,1)} %w_ref.1) | copy-start | bytes 2654212
  1.9 13.2 %collective-permute-start = (bf16[192,1152]{1,0:T(8,128)(2,1)S(1)}, bf16[192,1152]{1,0:T(8,128)(2,1)S(1)}, u32[]{:S(2)}, u32[]{:S(2)}) collective-permute-start(bf16[192,1152]{1,0:T(8,128)(2,1)S(1)} %take_half.1.refs_0_), channel_id=1, source_target_pairs={{0,4},{4,0},{8,12},{12,8},{16,20},{20,16},{24,28},{28,24},{1,5},{5... | collective-permute-start | bytes 1327112 | tf_op jit(solution)/shard_map/half_across/ppermute | solution.py:421
  4.5 12.2 %collective-permute-start.1 = (bf16[192,1152]{1,0:T(8,128)(2,1)S(1)}, bf16[192,1152]{1,0:T(8,128)(2,1)S(1)}, u32[]{:S(2)}, u32[]{:S(2)}) collective-permute-start(bf16[192,1152]{1,0:T(8,128)(2,1)S(1)} %take_half.1.refs_0_), channel_id=1, source_target_pairs={{8,0},{12,4},{16,24},{20,28},{0,8},{4,12},{24,16},{28,20},{9,1},{1... | collective-permute-start | bytes 1327112 | tf_op jit(solution)/shard_map/near/ppermute | solution.py:415
  6.1 10.6 %collective-permute-start.2 = (bf16[192,1152]{1,0:T(8,128)(2,1)S(1)}, bf16[192,1152]{1,0:T(8,128)(2,1)S(1)}, u32[]{:S(2)}, u32[]{:S(2)}) collective-permute-start(bf16[192,1152]{1,0:T(8,128)(2,1)S(1)} %take_half.1.refs_0_), channel_id=1, source_target_pairs={{8,16},{12,20},{16,8},{20,12},{9,17},{13,21},{17,9},{21,13},{10,18... | collective-permute-start | bytes 1327112 | tf_op jit(solution)/shard_map/mid/ppermute | solution.py:415
  16.6 15.4 %collective-permute-start.4 = (bf16[192,1152]{1,0:T(8,128)(2,1)S(1)}, bf16[192,1152]{1,0:T(8,128)(2,1)S(1)}, u32[]{:S(2)}, u32[]{:S(2)}) collective-permute-start(bf16[192,1152]{1,0:T(8,128)(2,1)S(1)} %collective-permute-done.2.between_ref), channel_id=1, source_target_pairs={{8,0},{12,4},{16,24},{20,28},{9,1},{13,5},{17,25},{21,29},{10,2},{... | collective-permute-start | bytes 1327112 | tf_op jit(solution)/shard_map/end_mid/ppermute | solution.py:415
  17.9 14.4 %collective-permute-start.3 = (bf16[192,1152]{1,0:T(8,128)(2,1)S(1)}, bf16[192,1152]{1,0:T(8,128)(2,1)S(1)}, u32[]{:S(2)}, u32[]{:S(2)}) collective-permute-start(bf16[192,1152]{1,0:T(8,128)(2,1)S(1)} %collective-permute-done.1.refs_2_), channel_id=1, source_target_pairs={{0,4},{4,0},{8,12},{12,8},{16,20},{20,16},{24,28},{28,24},{1,5},{5... | collective-permute-start | bytes 1327112 | tf_op jit(solution)/shard_map/near_across/ppermute | solution.py:421
  18.3 14.6 %collective-permute-start.6 = (bf16[192,1152]{1,0:T(8,128)(2,1)S(1)}, bf16[192,1152]{1,0:T(8,128)(2,1)S(1)}, u32[]{:S(2)}, u32[]{:S(2)}) collective-permute-start(bf16[192,1152]{1,0:T(8,128)(2,1)S(1)} %collective-permute-done.1.refs_2_), channel_id=1, source_target_pairs={{8,16},{12,20},{16,8},{20,12},{9,17},{13,21},{17,9},{21,13},{10,18... | collective-permute-start | bytes 1327112 | tf_op jit(solution)/shard_map/mid_far/ppermute | solution.py:415
  32.3 10.7 %collective-permute-start.5 = (bf16[192,1152]{1,0:T(8,128)(2,1)S(1)}, bf16[192,1152]{1,0:T(8,128)(2,1)S(1)}, u32[]{:S(2)}, u32[]{:S(2)}) collective-permute-start(bf16[192,1152]{1,0:T(8,128)(2,1)S(1)} %choose.2.refs_4_), channel_id=1, source_target_pairs={{0,4},{4,0},{8,12},{12,8},{16,20},{20,16},{24,28},{28,24},{1,5},{5... | collective-permute-start | bytes 1327112 | tf_op jit(solution)/shard_map/second_across/ppermute | solution.py:421
  32.9 12.8 %collective-permute-start.7 = (bf16[192,1152]{1,0:T(8,128)(2,1)S(1)}, bf16[192,1152]{1,0:T(8,128)(2,1)S(1)}, u32[]{:S(2)}, u32[]{:S(2)}) collective-permute-start(bf16[192,1152]{1,0:T(8,128)(2,1)S(1)} %collective-permute-done.6.between_ref), channel_id=1, source_target_pairs={{8,0},{12,4},{16,24},{20,28},{9,1},{13,5},{17,25},{21,29},{10,2},{... | collective-permute-start | bytes 1327112 | tf_op jit(solution)/shard_map/end_far/ppermute | solution.py:415
  34.4 21.8 %collective-permute-start.10 = (bf16[256,1536]{1,0:T(8,128)(2,1)S(1)}, bf16[256,1536]{1,0:T(8,128)(2,1)S(1)}, u32[]{:S(2)}, u32[]{:S(2)}) collective-permute-start(bf16[256,1536]{1,0:T(8,128)(2,1)S(1)} %get-tuple-element.29), channel_id=1, source_target_pairs={{1,3},{5,7},{9,11},{13,15},{17,19},{21,23},{25,27},{29,31}} | collective-permute-start | bytes 2359304 | tf_op jit(solution)/shard_map/halo/ppermute | solution.py:485
  45.7 11.8 %collective-permute-start.11 = (bf16[256,1536]{1,0:T(8,128)(2,1)S(1)}, bf16[256,1536]{1,0:T(8,128)(2,1)S(1)}, u32[]{:S(2)}, u32[]{:S(2)}) collective-permute-start(bf16[256,1536]{1,0:T(8,128)(2,1)S(1)} %get-tuple-element.31), channel_id=1, source_target_pairs={{1,3},{5,7},{9,11},{13,15},{17,19},{21,23},{25,27},{29,31}} | collective-permute-start | bytes 2359304 | tf_op jit(solution)/shard_map/halo/ppermute | solution.py:485
  46.7 12.1 %copy-start.2 = (s32[1,3]{1,0:T(1,128)S(1)}, s32[1,3]{1,0:T(1,128)}, u32[]{:S(2)}) copy-start(s32[1,3]{1,0:T(1,128)} %start_ref.3) | copy-start | bytes 40
  46.7 12.1 %copy-start.3 = (s32[1,12]{1,0:T(1,128)S(1)}, s32[1,12]{1,0:T(1,128)}, u32[]{:S(2)}) copy-start(s32[1,12]{1,0:T(1,128)} %owner_ref.3) | copy-start | bytes 148
  46.7 12.1 %copy-start.4 = (s32[1,12]{1,0:T(1,128)S(1)}, s32[1,12]{1,0:T(1,128)}, u32[]{:S(2)}) copy-start(s32[1,12]{1,0:T(1,128)} %left_ref.3) | copy-start | bytes 148
  46.7 12.0 %collective-permute-start.8 = (bf16[192,1152]{1,0:T(8,128)(2,1)S(1)}, bf16[192,1152]{1,0:T(8,128)(2,1)S(1)}, u32[]{:S(2)}, u32[]{:S(2)}) collective-permute-start(bf16[192,1152]{1,0:T(8,128)(2,1)S(1)} %choose.3.refs_6_), channel_id=1, source_target_pairs={{0,4},{4,0},{8,12},{12,8},{16,20},{20,16},{24,28},{28,24},{1,5},{5... | collective-permute-start | bytes 1327112 | tf_op jit(solution)/shard_map/third_across/ppermute | solution.py:421
  56.1 13.4 %collective-permute-start.12 = (bf16[256,1536]{1,0:T(8,128)(2,1)S(1)}, bf16[256,1536]{1,0:T(8,128)(2,1)S(1)}, u32[]{:S(2)}, u32[]{:S(2)}) collective-permute-start(bf16[256,1536]{1,0:T(8,128)(2,1)S(1)} %collective-permute-done.10.refs_10_), channel_id=1, source_target_pairs={{1,0},{3,2},{5,4},{7,6},{9,8},{11,10},{13,12},{15,14},{17,16},{19,... | collective-permute-start | bytes 2359304 | tf_op jit(solution)/shard_map/halo_first/ppermute | solution.py:491
  57.4 12.0 %collective-permute-start.13 = (bf16[256,1536]{1,0:T(8,128)(2,1)S(1)}, bf16[256,1536]{1,0:T(8,128)(2,1)S(1)}, u32[]{:S(2)}, u32[]{:S(2)}) collective-permute-start(bf16[256,1536]{1,0:T(8,128)(2,1)S(1)} %collective-permute-done.11.refs_11_), channel_id=1, source_target_pairs={{1,0},{3,2},{5,4},{7,6},{9,8},{11,10},{13,12},{15,14},{17,16},{19,... | collective-permute-start | bytes 2359304 | tf_op jit(solution)/shard_map/halo_first/ppermute | solution.py:491
  67.6 6.3 %collective-permute-start.14 = (bf16[1024,384]{1,0:T(8,128)(2,1)S(1)}, bf16[1024,384]{1,0:T(8,128)(2,1)S(1)}, u32[]{:S(2)}, u32[]{:S(2)}) collective-permute-start(bf16[1024,384]{1,0:T(8,128)(2,1)S(1)} %get-tuple-element.40.refs_2_), channel_id=1, source_target_pairs={{0,1},{1,0},{2,3},{3,2},{4,5},{5,4},{6,7},{7,6},{8,9},{9,8},{10,11... | collective-permute-start | bytes 2359304 | tf_op jit(solution)/shard_map/swap/ppermute | solution.py:496
where the time goes:
time: 75 us; the launch traced here: 75.1 us
  waiting for transfers between devices  33.6 us (45%)
  Pallas kernels  22.8 us (30%)
  starting transfers between devices  17 us (23%)
  local copies, waits for them, and re-layouts  1.42 us (2%)
    ppermute x5, waiting for transfers between devices, along(): lax.ppermute(block, 'dp', [(2 * a + s, 2 * b + s) for a, b in hops for s...  17.1 us
    ppermute x4, waiting for transfers between devices, across(): lax.ppermute(block, 'dp', [(2 * a + s, 2 * a + 1 - s) for a in places for...  16.5 us
    pallas_call x1, Pallas kernels, project_late_attend(): pl.pallas_call(functools.partial(late_kernel, blocks), out_shape=[jax.Sha...  8.8 us
    pallas_call x1, Pallas kernels, project_early(): pl.pallas_call(functools.partial(early_kernel, blocks), out_shape=[jax.Sh...  7.82 us
    ppermute x5, starting transfers between devices, along(): lax.ppermute(block, 'dp', [(2 * a + s, 2 * b + s) for a, b in hops for s...  5.49 us
    ppermute x4, starting transfers between devices, across(): lax.ppermute(block, 'dp', [(2 * a + s, 2 * a + 1 - s) for a in places for...  5.12 us
    pallas_call x1, Pallas kernels, attend_own(): pl.pallas_call(own_kernel, out_shape=jax.ShapeDtypeStruct((rows, width),...  4.42 us
    ppermute x2, starting transfers between devices, local(): halo_first = [lax.ppermute(after(x, *sums), 'tm', back) for x in halo]  2.58 us
  transfers between devices with their start and end apart: 15, of which 5 were waited for; matrix products, arithmetic and copies ran while one was open for 0% of the time, Pallas kernels for 29%

commit v1 on v0

--- a/solution.py
+++ b/solution.py
@@ -73,21 +73,21 @@
     columns = pl.ds(pl.multiple_of(first, LANES), depth)
     pairs.append((own_ref.at[:, columns], own_s))
     pairs.append((partner_ref.at[:, columns], partner_s))
-    for copy in start_all(sems, pairs):
-        copy.wait()
-    width = w_s.shape[1] // 3
-    for x_s, out in ((own_s, own_sum), (partner_s, partner_sum)):
-        for third in range(3):
-            cols = slice(third * width, (third + 1) * width)
-            out[:, cols] = dot(x_s[...], w_s[:, cols])
+    *first_copies, last_copy = start_all(sems, pairs)
+    for copy in first_copies:
+        copy.wait()
+    own_sum[...] = dot(own_s[...], w_s[...])
+    last_copy.wait()
+    partner_sum[...] = dot(partner_s[...], w_s[...])
 
 
 def project_halo(halo_refs, kv_ref, k_ref, v_ref):
     width = k_ref.shape[1]
     for i, frames_ref in enumerate(halo_refs):
         at = slice(i * STRETCH, (i + 1) * STRETCH)
-        k_ref[at, :] = dot(frames_ref[...], kv_ref[:, :width]).astype(jnp.bfloat16)
-        v_ref[at, :] = dot(frames_ref[...], kv_ref[:, width:]).astype(jnp.bfloat16)
+        both = dot(frames_ref[...], kv_ref[...]).astype(jnp.bfloat16)
+        k_ref[at, :] = both[:, :width]
+        v_ref[at, :] = both[:, width:]
 
 
 def late_kernel(blocks, start_ref, owner_ref, left_ref, *refs):
@@ -109,14 +109,16 @@
     n_first = len(pairs)
     pairs += blocks.copies(refs, found, everything, kv_out, 0, slice(width, 3 * width))
     copies = start_all(sems, pairs)
-    for copy in copies[:n_first]:
+    for copy in copies[: n_first - 1]:
         copy.wait()
     for x_s, acc, place in ((partner_s, partner_sum, 1 - core), (own_s, own_sum, core)):
+        if x_s is own_s:
+            copies[n_first - 1].wait()
         row = pl.multiple_of(place * rows, STRETCH)
+        value = (acc[...] + dot(x_s[...], w_s[...])).astype(jnp.bfloat16)
         for third, (dst, skip) in enumerate(((q_out, 0), (k_out, REACH), (v_out, REACH))):
-            cols = slice(third * width, (third + 1) * width)
-            value = (acc[:, cols] + dot(x_s[...], w_s[:, cols])).astype(jnp.bfloat16)
-            dst[pl.ds(pl.multiple_of(row + skip, STRETCH), rows), :] = value
+            part = value[:, third * width : (third + 1) * width]
+            dst[pl.ds(pl.multiple_of(row + skip, STRETCH), rows), :] = part
     for copy in copies[n_first:]:
         copy.wait()
 

time: 75 us -> 74.2 us (0.989)
  starting transfers between devices: 17 us -> 16.1 us
    ppermute x1, starting transfers between devices: 1.9 us -> 1.08 us  [local(): other = lax.ppermute(attended, 'tm', [(i, i ^ 1) for i in range(members)])]
where the time goes in v1:
time: 74.2 us; the launch traced here: 74.4 us
  waiting for transfers between devices  33.6 us (45%)
  Pallas kernels  22.9 us (31%)
  starting transfers between devices  16.1 us (22%)
  local copies, waits for them, and re-layouts  1.42 us (2%)
    ppermute x5, waiting for transfers between devices, along(): lax.ppermute(block, 'dp', [(2 * a + s, 2 * b + s) for a, b in hops for s...  17.1 us
    ppermute x4, waiting for transfers between devices, across(): lax.ppermute(block, 'dp', [(2 * a + s, 2 * a + 1 - s) for a in places for...  16.5 us
    pallas_call x1, Pallas kernels, project_late_attend(): pl.pallas_call(functools.partial(late_kernel, blocks), out_shape=[jax.Sha...  9.07 us
    pallas_call x1, Pallas kernels, project_early(): pl.pallas_call(functools.partial(early_kernel, blocks), out_shape=[jax.Sh...  7.87 us
    ppermute x5, starting transfers between devices, along(): lax.ppermute(block, 'dp', [(2 * a + s, 2 * b + s) for a, b in hops for s...  5.49 us
    ppermute x4, starting transfers between devices, across(): lax.ppermute(block, 'dp', [(2 * a + s, 2 * a + 1 - s) for a in places for...  5.12 us
    pallas_call x1, Pallas kernels, attend_own(): pl.pallas_call(own_kernel, out_shape=jax.ShapeDtypeStruct((rows, width),...  4.2 us
    ppermute x2, starting transfers between devices, local(): halo_first = [lax.ppermute(after(x, *sums), 'tm', back) for x in halo]  2.58 us
  transfers between devices with their start and end apart: 15, of which 5 were waited for; matrix products, arithmetic and copies ran while one was open for 0% of the time, Pallas kernels for 29%

profile of v1, /device:TPU:0, one launch (start us, length us, event | category | flops | bytes accessed | tf_op | source)
XLA Modules:
  0.0 74.4 jit_solution(16745227666671680787)
XLA Ops:
  0.0 0.0 copy-start
  0.0 0.5 collective-permute-start.9
  0.5 0.0 copy-start.1
  0.5 1.4 %copy-done.1 = bf16[192,2304]{1,0:T(8,128)(2,1)S(1)} copy-done((bf16[192,2304]{1,0:T(8,128)(2,1)S(1)}, bf16[192,2304]{1,0:T(8,128)(2,1)}, u32[]{:S(2)}) %copy-start.1) | copy-done | bytes 884760
  1.9 0.1 take_half.1.refs_0_
  1.9 2.5 %collective-permute-start = (bf16[192,1152]{1,0:T(8,128)(2,1)S(1)}, bf16[192,1152]{1,0:T(8,128)(2,1)S(1)}, u32[]{:S(2)}, u32[]{:S(2)}) collective-permute-start(bf16[192,1152]{1,0:T(8,128)(2,1)S(1)} %take_half.1.refs_0_), channel_id=1, source_target_pairs={{0,4},{4,0},{8,12},{12,8},{16,20},{20,16},{24,28},{28,24},{1,5},{5... | collective-permute-start | bytes 1327112 | tf_op jit(solution)/shard_map/half_across/ppermute | solution.py:423
  4.5 1.6 %collective-permute-start.1 = (bf16[192,1152]{1,0:T(8,128)(2,1)S(1)}, bf16[192,1152]{1,0:T(8,128)(2,1)S(1)}, u32[]{:S(2)}, u32[]{:S(2)}) collective-permute-start(bf16[192,1152]{1,0:T(8,128)(2,1)S(1)} %take_half.1.refs_0_), channel_id=1, source_target_pairs={{8,0},{12,4},{16,24},{20,28},{0,8},{4,12},{24,16},{28,20},{9,1},{1... | collective-permute-start | bytes 1327112 | tf_op jit(solution)/shard_map/near/ppermute | solution.py:417
  6.1 0.7 collective-permute-start.2
  6.7 8.4 %collective-permute-done.refs_1_ = bf16[192,1152]{1,0:T(8,128)(2,1)S(1)} collective-permute-done((bf16[192,1152]{1,0:T(8,128)(2,1)S(1)}, bf16[192,1152]{1,0:T(8,128)(2,1)S(1)}, u32[]{:S(2)}, u32[]{:S(2)}) %collective-permute-start) | collective-permute-done | bytes 442400 | tf_op jit(solution)/shard_map/half_across/ppermute | solution.py:423
  15.2 1.5 %collective-permute-done.1.refs_2_ = bf16[192,1152]{1,0:T(8,128)(2,1)S(1)} collective-permute-done((bf16[192,1152]{1,0:T(8,128)(2,1)S(1)}, bf16[192,1152]{1,0:T(8,128)(2,1)S(1)}, u32[]{:S(2)}, u32[]{:S(2)}) %collective-permute-start.1) | collective-permute-done | bytes 442400 | tf_op jit(solution)/shard_map/near/ppermute | solution.py:417
  16.6 0.0 collective-permute-done.2.between_ref
  16.6 1.3 %collective-permute-start.4 = (bf16[192,1152]{1,0:T(8,128)(2,1)S(1)}, bf16[192,1152]{1,0:T(8,128)(2,1)S(1)}, u32[]{:S(2)}, u32[]{:S(2)}) collective-permute-start(bf16[192,1152]{1,0:T(8,128)(2,1)S(1)} %collective-permute-done.2.between_ref), channel_id=1, source_target_pairs={{8,0},{12,4},{16,24},{20,28},{9,1},{13,5},{17,25},{21,29},{10,2},{... | collective-permute-start | bytes 1327112 | tf_op jit(solution)/shard_map/end_mid/ppermute | solution.py:417
  17.9 0.4 collective-permute-start.3
  18.3 0.7 collective-permute-start.6
  19.0 13.0 %collective-permute-done.4.end_ref = bf16[192,1152]{1,0:T(8,128)(2,1)S(1)} collective-permute-done((bf16[192,1152]{1,0:T(8,128)(2,1)S(1)}, bf16[192,1152]{1,0:T(8,128)(2,1)S(1)}, u32[]{:S(2)}, u32[]{:S(2)}) %collective-permute-start.4) | collective-permute-done | bytes 442400 | tf_op jit(solution)/shard_map/end_mid/ppermute | solution.py:417
  32.1 0.3 choose.2.refs_4_
  32.3 0.0 collective-permute-done.3.refs_3_
  32.3 0.6 collective-permute-start.5
  32.9 0.0 collective-permute-done.6.between_ref
  32.9 1.3 %collective-permute-start.7 = (bf16[192,1152]{1,0:T(8,128)(2,1)S(1)}, bf16[192,1152]{1,0:T(8,128)(2,1)S(1)}, u32[]{:S(2)}, u32[]{:S(2)}) collective-permute-start(bf16[192,1152]{1,0:T(8,128)(2,1)S(1)} %collective-permute-done.6.between_ref), channel_id=1, source_target_pairs={{8,0},{12,4},{16,24},{20,28},{9,1},{13,5},{17,25},{21,29},{10,2},{... | collective-permute-start | bytes 1327112 | tf_op jit(solution)/shard_map/end_far/ppermute | solution.py:417
  34.2 0.0 copy-done
  34.2 0.1 take_tail.1
  34.4 0.7 collective-permute-start.10
  35.1 8.0 %collective-permute-done.5.refs_5_ = bf16[192,1152]{1,0:T(8,128)(2,1)S(1)} collective-permute-done((bf16[192,1152]{1,0:T(8,128)(2,1)S(1)}, bf16[192,1152]{1,0:T(8,128)(2,1)S(1)}, u32[]{:S(2)}, u32[]{:S(2)}) %collective-permute-start.5) | collective-permute-done | bytes 442400 | tf_op jit(solution)/shard_map/second_across/ppermute | solution.py:423
  43.1 2.6 %collective-permute-done.7.end_ref = bf16[192,1152]{1,0:T(8,128)(2,1)S(1)} collective-permute-done((bf16[192,1152]{1,0:T(8,128)(2,1)S(1)}, bf16[192,1152]{1,0:T(8,128)(2,1)S(1)}, u32[]{:S(2)}, u32[]{:S(2)}) %collective-permute-start.7) | collective-permute-done | bytes 442400 | tf_op jit(solution)/shard_map/end_far/ppermute | solution.py:417
  45.7 0.7 collective-permute-start.11
  46.4 0.3 choose.3.refs_6_
  46.7 0.0 copy-start.2
  46.7 0.0 copy-start.3
  46.7 0.0 copy-start.4
  46.7 1.6 %collective-permute-start.8 = (bf16[192,1152]{1,0:T(8,128)(2,1)S(1)}, bf16[192,1152]{1,0:T(8,128)(2,1)S(1)}, u32[]{:S(2)}, u32[]{:S(2)}) collective-permute-start(bf16[192,1152]{1,0:T(8,128)(2,1)S(1)} %choose.3.refs_6_), channel_id=1, source_target_pairs={{0,4},{4,0},{8,12},{12,8},{16,20},{20,16},{24,28},{28,24},{1,5},{5... | collective-permute-start | bytes 1327112 | tf_op jit(solution)/shard_map/third_across/ppermute | solution.py:423
  48.3 0.0 collective-permute-done.9.refs_7_.refs_9_
  48.3 7.9 %project_early.1 = (f32[768,1152]{1,0:T(8,128)S(1)}, f32[768,1152]{1,0:T(8,128)S(1)}) custom-call(bf16[192,1152]{1,0:T(8,128)(2,1)S(1)} %take_half.1.refs_0_, bf16[192,1152]{1,0:T(8,128)(2,1)S(1)} %collective-permute-done.refs_1_, bf16[192,1152]{1,0:T(8,128)(2,1)S(1)} %collective-permute-done.1.refs_2_, ...), custom_call_target="tpu_custom_call" | custom-call | tf_op jit(solution)/shard_map/project_early/pallas_call | solution.py:308
  56.2 0.0 collective-permute-done.10.refs_10_
  56.2 1.3 %collective-permute-start.12 = (bf16[256,1536]{1,0:T(8,128)(2,1)S(1)}, bf16[256,1536]{1,0:T(8,128)(2,1)S(1)}, u32[]{:S(2)}, u32[]{:S(2)}) collective-permute-start(bf16[256,1536]{1,0:T(8,128)(2,1)S(1)} %collective-permute-done.10.refs_10_), channel_id=1, source_target_pairs={{1,0},{3,2},{5,4},{7,6},{9,8},{11,10},{13,12},{15,14},{17,16},{19,... | collective-permute-start | bytes 2359304 | tf_op jit(solution)/shard_map/halo_first/ppermute | solution.py:493
  57.5 0.0 collective-permute-done.11.refs_11_
  57.5 1.3 %collective-permute-start.13 = (bf16[256,1536]{1,0:T(8,128)(2,1)S(1)}, bf16[256,1536]{1,0:T(8,128)(2,1)S(1)}, u32[]{:S(2)}, u32[]{:S(2)}) collective-permute-start(bf16[256,1536]{1,0:T(8,128)(2,1)S(1)} %collective-permute-done.11.refs_11_), channel_id=1, source_target_pairs={{1,0},{3,2},{5,4},{7,6},{9,8},{11,10},{13,12},{15,14},{17,16},{19,... | collective-permute-start | bytes 2359304 | tf_op jit(solution)/shard_map/halo_first/ppermute | solution.py:493
  58.8 0.0 collective-permute-done.8.refs_7_
  58.8 0.0 copy-done.2
  58.8 0.0 copy-done.3
  58.8 0.0 copy-done.4
  58.8 9.1 %project_late_attend.1 = (bf16[1024,384]{1,0:T(8,128)(2,1)S(1)}, bf16[1536,384]{1,0:T(8,128)(2,1)S(1)}, bf16[2048,384]{1,0:T(8,128)(2,1)S(1)}, bf16[2048,384]{1,0:T(8,128)(2,1)S(1)}, bf16[1536,768]{1,0:T(8,128)(2,1)S(1)}) custom-call(s32[1,3]{1,0:T(1,128)S(1)} %copy-done.2, s32[1,12]{1,0:T(1,128)S(1)} %copy-done.3, s32[1,12]{1,0:T(1,128)S(1)} %copy-done.4, ...), custom_call_target="tpu_custom_call" | custom-call | tf_op jit(solution)/shard_map/project_late_attend/pallas_call | solution.py:354
  67.9 1.1 %collective-permute-start.14 = (bf16[1024,384]{1,0:T(8,128)(2,1)S(1)}, bf16[1024,384]{1,0:T(8,128)(2,1)S(1)}, u32[]{:S(2)}, u32[]{:S(2)}) collective-permute-start(bf16[1024,384]{1,0:T(8,128)(2,1)S(1)} %get-tuple-element.40.refs_2_), channel_id=1, source_target_pairs={{0,1},{1,0},{2,3},{3,2},{4,5},{5,4},{6,7},{7,6},{8,9},{9,8},{10,11... | collective-permute-start | bytes 2359304 | tf_op jit(solution)/shard_map/swap/ppermute | solution.py:498
  69.0 0.0 collective-permute-done.12.refs_0_
  69.0 0.0 collective-permute-done.13.refs_1_
  69.0 4.2 %attend_own.1.own_ref = bf16[768,384]{1,0:T(8,128)(2,1)S(1)} custom-call(s32[1,3]{1,0:T(1,128)S(1)} %copy-done.2, s32[1,12]{1,0:T(1,128)S(1)} %copy-done.3, s32[1,12]{1,0:T(1,128)S(1)} %copy-done.4, bf16[1536,384]{1,0:T(8,128)(2,1)S(1)} %get-tuple-element.34.q_ref, bf16[2048,384]{1,0:T(8,128)(2,1)S(1)} %get-tuple-element.35.k_ref, ...), custom_call_target="tpu_custom_call" | custom-call | tf_op jit(solution)/shard_map/attend_own/pallas_call | solution.py:379
  73.2 0.0 collective-permute-done.14.other_ref
  73.2 1.0 %join.1 = bf16[768,768]{1,0:T(8,128)(2,1)} custom-call(bf16[768,384]{1,0:T(8,128)(2,1)S(1)} %attend_own.1.own_ref, bf16[1024,384]{1,0:T(8,128)(2,1)S(1)} %collective-permute-done.14.other_ref), custom_call_target="tpu_custom_call" | custom-call | tf_op jit(solution)/shard_map/join/pallas_call | solution.py:292
Async XLA Ops:
  0.0 34.2 %copy-start = (bf16[1,768,1536]{2,1,0:T(8,128)(2,1)S(1)}, bf16[1,768,1536]{2,1,0:T(8,128)(2,1)}, u32[]{:S(2)}) copy-start(bf16[1,768,1536]{2,1,0:T(8,128)(2,1)} %param.5) | copy-start | bytes 7077892
  0.0 48.3 %collective-permute-start.9 = (bf16[768,1536]{1,0:T(8,128)(2,1)}, bf16[768,1536]{1,0:T(8,128)(2,1)S(1)}, u32[]{:S(2)}, u32[]{:S(2)}) collective-permute-start(bf16[768,1536]{1,0:T(8,128)(2,1)} %bitcast.2), channel_id=1, source_target_pairs={{0,1},{1,0},{2,3},{3,2},{4,5},{5,4},{6,7},{7,6},{8,9},{9,8},{10,11... | collective-permute-start | bytes 7077896 | tf_op jit(solution)/shard_map/partner/ppermute | solution.py:475
  0.5 1.4 %copy-start.1 = (bf16[192,2304]{1,0:T(8,128)(2,1)S(1)}, bf16[192,2304]{1,0:T(8,128)(2,1)}, u32[]{:S(2)}) copy-start(bf16[192,2304]{1,0:T(8,128)(2,1)} %w_ref.1) | copy-start | bytes 2654212
  1.9 13.2 %collective-permute-start = (bf16[192,1152]{1,0:T(8,128)(2,1)S(1)}, bf16[192,1152]{1,0:T(8,128)(2,1)S(1)}, u32[]{:S(2)}, u32[]{:S(2)}) collective-permute-start(bf16[192,1152]{1,0:T(8,128)(2,1)S(1)} %take_half.1.refs_0_), channel_id=1, source_target_pairs={{0,4},{4,0},{8,12},{12,8},{16,20},{20,16},{24,28},{28,24},{1,5},{5... | collective-permute-start | bytes 1327112 | tf_op jit(solution)/shard_map/half_across/ppermute | solution.py:423
  4.5 12.2 %collective-permute-start.1 = (bf16[192,1152]{1,0:T(8,128)(2,1)S(1)}, bf16[192,1152]{1,0:T(8,128)(2,1)S(1)}, u32[]{:S(2)}, u32[]{:S(2)}) collective-permute-start(bf16[192,1152]{1,0:T(8,128)(2,1)S(1)} %take_half.1.refs_0_), channel_id=1, source_target_pairs={{8,0},{12,4},{16,24},{20,28},{0,8},{4,12},{24,16},{28,20},{9,1},{1... | collective-permute-start | bytes 1327112 | tf_op jit(solution)/shard_map/near/ppermute | solution.py:417
  6.1 10.6 %collective-permute-start.2 = (bf16[192,1152]{1,0:T(8,128)(2,1)S(1)}, bf16[192,1152]{1,0:T(8,128)(2,1)S(1)}, u32[]{:S(2)}, u32[]{:S(2)}) collective-permute-start(bf16[192,1152]{1,0:T(8,128)(2,1)S(1)} %take_half.1.refs_0_), channel_id=1, source_target_pairs={{8,16},{12,20},{16,8},{20,12},{9,17},{13,21},{17,9},{21,13},{10,18... | collective-permute-start | bytes 1327112 | tf_op jit(solution)/shard_map/mid/ppermute | solution.py:417
  16.6 15.4 %collective-permute-start.4 = (bf16[192,1152]{1,0:T(8,128)(2,1)S(1)}, bf16[192,1152]{1,0:T(8,128)(2,1)S(1)}, u32[]{:S(2)}, u32[]{:S(2)}) collective-permute-start(bf16[192,1152]{1,0:T(8,128)(2,1)S(1)} %collective-permute-done.2.between_ref), channel_id=1, source_target_pairs={{8,0},{12,4},{16,24},{20,28},{9,1},{13,5},{17,25},{21,29},{10,2},{... | collective-permute-start | bytes 1327112 | tf_op jit(solution)/shard_map/end_mid/ppermute | solution.py:417
  17.9 14.4 %collective-permute-start.3 = (bf16[192,1152]{1,0:T(8,128)(2,1)S(1)}, bf16[192,1152]{1,0:T(8,128)(2,1)S(1)}, u32[]{:S(2)}, u32[]{:S(2)}) collective-permute-start(bf16[192,1152]{1,0:T(8,128)(2,1)S(1)} %collective-permute-done.1.refs_2_), channel_id=1, source_target_pairs={{0,4},{4,0},{8,12},{12,8},{16,20},{20,16},{24,28},{28,24},{1,5},{5... | collective-permute-start | bytes 1327112 | tf_op jit(solution)/shard_map/near_across/ppermute | solution.py:423
  18.3 14.6 %collective-permute-start.6 = (bf16[192,1152]{1,0:T(8,128)(2,1)S(1)}, bf16[192,1152]{1,0:T(8,128)(2,1)S(1)}, u32[]{:S(2)}, u32[]{:S(2)}) collective-permute-start(bf16[192,1152]{1,0:T(8,128)(2,1)S(1)} %collective-permute-done.1.refs_2_), channel_id=1, source_target_pairs={{8,16},{12,20},{16,8},{20,12},{9,17},{13,21},{17,9},{21,13},{10,18... | collective-permute-start | bytes 1327112 | tf_op jit(solution)/shard_map/mid_far/ppermute | solution.py:417
  32.3 10.7 %collective-permute-start.5 = (bf16[192,1152]{1,0:T(8,128)(2,1)S(1)}, bf16[192,1152]{1,0:T(8,128)(2,1)S(1)}, u32[]{:S(2)}, u32[]{:S(2)}) collective-permute-start(bf16[192,1152]{1,0:T(8,128)(2,1)S(1)} %choose.2.refs_4_), channel_id=1, source_target_pairs={{0,4},{4,0},{8,12},{12,8},{16,20},{20,16},{24,28},{28,24},{1,5},{5... | collective-permute-start | bytes 1327112 | tf_op jit(solution)/shard_map/second_across/ppermute | solution.py:423
  32.9 12.8 %collective-permute-start.7 = (bf16[192,1152]{1,0:T(8,128)(2,1)S(1)}, bf16[192,1152]{1,0:T(8,128)(2,1)S(1)}, u32[]{:S(2)}, u32[]{:S(2)}) collective-permute-start(bf16[192,1152]{1,0:T(8,128)(2,1)S(1)} %collective-permute-done.6.between_ref), channel_id=1, source_target_pairs={{8,0},{12,4},{16,24},{20,28},{9,1},{13,5},{17,25},{21,29},{10,2},{... | collective-permute-start | bytes 1327112 | tf_op jit(solution)/shard_map/end_far/ppermute | solution.py:417
  34.4 21.8 %collective-permute-start.10 = (bf16[256,1536]{1,0:T(8,128)(2,1)S(1)}, bf16[256,1536]{1,0:T(8,128)(2,1)S(1)}, u32[]{:S(2)}, u32[]{:S(2)}) collective-permute-start(bf16[256,1536]{1,0:T(8,128)(2,1)S(1)} %get-tuple-element.29), channel_id=1, source_target_pairs={{1,3},{5,7},{9,11},{13,15},{17,19},{21,23},{25,27},{29,31}} | collective-permute-start | bytes 2359304 | tf_op jit(solution)/shard_map/halo/ppermute | solution.py:487
  45.7 11.8 %collective-permute-start.11 = (bf16[256,1536]{1,0:T(8,128)(2,1)S(1)}, bf16[256,1536]{1,0:T(8,128)(2,1)S(1)}, u32[]{:S(2)}, u32[]{:S(2)}) collective-permute-start(bf16[256,1536]{1,0:T(8,128)(2,1)S(1)} %get-tuple-element.31), channel_id=1, source_target_pairs={{1,3},{5,7},{9,11},{13,15},{17,19},{21,23},{25,27},{29,31}} | collective-permute-start | bytes 2359304 | tf_op jit(solution)/shard_map/halo/ppermute | solution.py:487
  46.7 12.1 %copy-start.2 = (s32[1,3]{1,0:T(1,128)S(1)}, s32[1,3]{1,0:T(1,128)}, u32[]{:S(2)}) copy-start(s32[1,3]{1,0:T(1,128)} %start_ref.3) | copy-start | bytes 40
  46.7 12.1 %copy-start.3 = (s32[1,12]{1,0:T(1,128)S(1)}, s32[1,12]{1,0:T(1,128)}, u32[]{:S(2)}) copy-start(s32[1,12]{1,0:T(1,128)} %owner_ref.3) | copy-start | bytes 148
  46.7 12.1 %copy-start.4 = (s32[1,12]{1,0:T(1,128)S(1)}, s32[1,12]{1,0:T(1,128)}, u32[]{:S(2)}) copy-start(s32[1,12]{1,0:T(1,128)} %left_ref.3) | copy-start | bytes 148
  46.7 12.1 %collective-permute-start.8 = (bf16[192,1152]{1,0:T(8,128)(2,1)S(1)}, bf16[192,1152]{1,0:T(8,128)(2,1)S(1)}, u32[]{:S(2)}, u32[]{:S(2)}) collective-permute-start(bf16[192,1152]{1,0:T(8,128)(2,1)S(1)} %choose.3.refs_6_), channel_id=1, source_target_pairs={{0,4},{4,0},{8,12},{12,8},{16,20},{20,16},{24,28},{28,24},{1,5},{5... | collective-permute-start | bytes 1327112 | tf_op jit(solution)/shard_map/third_across/ppermute | solution.py:423
  56.2 12.8 %collective-permute-start.12 = (bf16[256,1536]{1,0:T(8,128)(2,1)S(1)}, bf16[256,1536]{1,0:T(8,128)(2,1)S(1)}, u32[]{:S(2)}, u32[]{:S(2)}) collective-permute-start(bf16[256,1536]{1,0:T(8,128)(2,1)S(1)} %collective-permute-done.10.refs_10_), channel_id=1, source_target_pairs={{1,0},{3,2},{5,4},{7,6},{9,8},{11,10},{13,12},{15,14},{17,16},{19,... | collective-permute-start | bytes 2359304 | tf_op jit(solution)/shard_map/halo_first/ppermute | solution.py:493
  57.5 11.5 %collective-permute-start.13 = (bf16[256,1536]{1,0:T(8,128)(2,1)S(1)}, bf16[256,1536]{1,0:T(8,128)(2,1)S(1)}, u32[]{:S(2)}, u32[]{:S(2)}) collective-permute-start(bf16[256,1536]{1,0:T(8,128)(2,1)S(1)} %collective-permute-done.11.refs_11_), channel_id=1, source_target_pairs={{1,0},{3,2},{5,4},{7,6},{9,8},{11,10},{13,12},{15,14},{17,16},{19,... | collective-permute-start | bytes 2359304 | tf_op jit(solution)/shard_map/halo_first/ppermute | solution.py:493
  67.9 5.3 %collective-permute-start.14 = (bf16[1024,384]{1,0:T(8,128)(2,1)S(1)}, bf16[1024,384]{1,0:T(8,128)(2,1)S(1)}, u32[]{:S(2)}, u32[]{:S(2)}) collective-permute-start(bf16[1024,384]{1,0:T(8,128)(2,1)S(1)} %get-tuple-element.40.refs_2_), channel_id=1, source_target_pairs={{0,1},{1,0},{2,3},{3,2},{4,5},{5,4},{6,7},{7,6},{8,9},{9,8},{10,11... | collective-permute-start | bytes 2359304 | tf_op jit(solution)/shard_map/swap/ppermute | solution.py:498

commit v2 on v1

--- a/solution.py
+++ b/solution.py
@@ -43,42 +43,46 @@
 
 
 class Blocks:
-    def __init__(self, blocks, n_late, find):
-        self.operands = [operand for block in blocks for operand in block]
-        self.counts = [len(block) for block in blocks]
-        self.rows = [block[0].shape[0] for block in blocks]
-        self.n_late = n_late
-        self.early_operands = self.operands[: sum(self.counts[:-n_late])]
+    def __init__(self, blocks, steps, find):
+        self.operands = list(blocks)
+        self.rows = [block.shape[0] for block in blocks]
+        self.steps = steps
         self.find = find
+
+    def step_operands(self, step):
+        return [self.operands[i] for i in self.steps[step]]
+
+    def step_depth(self, step):
+        return sum(self.rows[i] for i in self.steps[step])
 
     def copies(self, refs, found, members, target, first=0, columns=slice(None)):
         pairs = []
-        for i in members:
-            at = sum(self.counts[:i])
-            choices = [ref.at[:, columns] for ref in refs[at : at + self.counts[i]]]
-            row, which = found[i]
-            goal = target.at[pl.ds(pl.multiple_of(row - first, self.rows[i]), self.rows[i])]
-            pairs.append((choices[0], goal) if len(choices) == 1 else (choices, which, goal))
+        for ref, i in zip(refs, members):
+            rows = self.rows[i]
+            goal = target.at[pl.ds(pl.multiple_of(found[i] - first, rows), rows)]
+            pairs.append((ref.at[:, columns], goal))
         return pairs
 
 
-def early_kernel(blocks, *refs):
-    n = len(blocks.early_operands)
-    own_ref, partner_ref, own_sum, partner_sum, w_s, own_s, partner_s, sems = refs[n:]
-    found, late_first = blocks.find()
+def early_kernel(blocks, step, *refs):
+    n = len(blocks.step_operands(step))
+    own_ref, partner_ref, *sums = refs[n : n + 2 + 2 * min(step, 1)]
+    own_out, partner_out, w_s, own_s, partner_s, sems = refs[n + 2 + len(sums) :]
+    found, firsts = blocks.find()
     depth = w_s.shape[0]
-    first = jnp.where(late_first == 0, own_ref.shape[1] - depth, 0)
-    members = range(len(found) - blocks.n_late)
-    pairs = blocks.copies(refs, found, members, w_s, first)
+    first = firsts[step]
+    pairs = blocks.copies(refs, found, blocks.steps[step], w_s, first)
     columns = pl.ds(pl.multiple_of(first, LANES), depth)
     pairs.append((own_ref.at[:, columns], own_s))
     pairs.append((partner_ref.at[:, columns], partner_s))
     *first_copies, last_copy = start_all(sems, pairs)
     for copy in first_copies:
         copy.wait()
-    own_sum[...] = dot(own_s[...], w_s[...])
+    own = dot(own_s[...], w_s[...])
+    own_out[...] = own + sums[0][...] if sums else own
     last_copy.wait()
-    partner_sum[...] = dot(partner_s[...], w_s[...])
+    partner = dot(partner_s[...], w_s[...])
+    partner_out[...] = partner + sums[1][...] if sums else partner
 
 
 def project_halo(halo_refs, kv_ref, k_ref, v_ref):
@@ -100,9 +104,10 @@
     width = w_s.shape[1] // 3
     rows = own_s.shape[0]
     core = lax.axis_index("tm") % 2
-    found, late_first = blocks.find()
+    found, (*_, late_first) = blocks.find()
     everything = range(len(found))
-    pairs = blocks.copies(refs, found, everything[-blocks.n_late :], w_s, late_first)
+    last = blocks.steps[-1]
+    pairs = blocks.copies([refs[i] for i in last], found, last, w_s, late_first)
     columns = pl.ds(pl.multiple_of(late_first, LANES), depth)
     pairs.append((partner_ref.at[:, columns], partner_s))
     pairs.append((own_ref.at[:, columns], own_s))
@@ -300,26 +305,26 @@
     )(own, other)
 
 
-def project_early(blocks, inputs, partner):
-    rows, depth = inputs.shape
-    depth -= depth // GROUPS
-    cols = blocks.operands[0].shape[1]
-    n_copies = len(blocks.counts) - blocks.n_late + 2
-    return pl.pallas_call(
-        functools.partial(early_kernel, blocks),
+def project_early(blocks, step, inputs, partner, sums=()):
+    rows = inputs.shape[0]
+    depth = blocks.step_depth(step)
+    operands = blocks.step_operands(step)
+    cols = operands[0].shape[1]
+    return pl.pallas_call(
+        functools.partial(early_kernel, blocks, step),
         out_shape=[jax.ShapeDtypeStruct((rows, cols), jnp.float32)] * 2,
-        in_specs=[ANY_SPEC] * (len(blocks.early_operands) + 2),
+        in_specs=[ANY_SPEC] * (len(operands) + 2) + [VMEM_SPEC] * len(sums),
         out_specs=[VMEM_SPEC] * 2,
         scratch_shapes=[
             pltpu.VMEM((depth, cols), jnp.bfloat16),
             pltpu.VMEM((rows, depth), jnp.bfloat16),
             pltpu.VMEM((rows, depth), jnp.bfloat16),
-            pltpu.SemaphoreType.DMA((n_copies,)),
+            pltpu.SemaphoreType.DMA((len(operands) + 2,)),
         ],
-        compiler_params=pltpu.CompilerParams(vmem_limit_bytes=24 * MIB),
+        compiler_params=pltpu.CompilerParams(vmem_limit_bytes=20 * MIB),
         cost_estimate=pl.CostEstimate(flops=0, bytes_accessed=0, transcendentals=0),
         name="project_early",
-    )(*blocks.early_operands, inputs, partner)
+    )(*operands, inputs, partner, *sums)
 
 
 def tail_kernel(x_ref, *refs):
@@ -347,7 +352,7 @@
 
 def project_late_attend(tables, blocks, inputs, partner, halo, sums):
     rows, depth = inputs.shape
-    late_depth = depth // GROUPS
+    late_depth = blocks.step_depth(-1)
     cols = blocks.operands[0].shape[1]
     width = cols // 3
     keys = jax.ShapeDtypeStruct((2 * rows + REACH, width), jnp.bfloat16)
@@ -366,7 +371,7 @@
             pltpu.VMEM((late_depth, cols), jnp.bfloat16),
             pltpu.VMEM((rows, late_depth), jnp.bfloat16),
             pltpu.VMEM((rows, late_depth), jnp.bfloat16),
-            pltpu.SemaphoreType.DMA((len(blocks.counts) + blocks.n_late + 2,)),
+            pltpu.SemaphoreType.DMA((len(blocks.operands) + len(blocks.steps[-1]) + 2,)),
         ],
         compiler_params=pltpu.CompilerParams(vmem_limit_bytes=24 * MIB),
         name="project_late_attend",
@@ -446,21 +451,21 @@
         second = jnp.where(is_end == 1, place ^ 2, 3 - place)
         third = jnp.where(is_end == 1, 3 - place, place ^ 2)
         spots = (place, place ^ 1, second, third)
-        found = [((2 * spot + (side ^ n)) * size, is_end) for spot in spots for n in range(2)]
-        return found, third * 2 * size
+        found = [(2 * spot + (side ^ n)) * size for spot in spots for n in range(2)]
+        return found, [place // 2 * 4 * size, second * 2 * size, third * 2 * size]
 
     blocks = [
-        (half,),
-        (half_across,),
-        (near,),
-        (near_across,),
-        (second,),
-        (second_across,),
-        (third,),
-        (third_across,),
+        half,
+        half_across,
+        near,
+        near_across,
+        second,
+        second_across,
+        third,
+        third_across,
     ]
     marks = (near_across, mid_far, end_mid), (second_across, end_far), (third_across,)
-    return Blocks(blocks, 2, find), marks
+    return Blocks(blocks, ((0, 1, 2, 3), (4, 5), (6, 7)), find), marks
 
 
 def local(frames, w_qkv, utt_start, stretch_utt, left_stretches):
@@ -477,17 +482,19 @@
         blocks, marks = gather_neighbours(half)
     else:
         weights = lax.all_gather(half, "dp", axis=0, tiled=True)
-        late_first = depth - depth // GROUPS
-        found = [(0, 0), (late_first, 0)], late_first
-        parts = [(weights[:late_first],), (weights[late_first:],)]
-        blocks, marks = Blocks(parts, 1, lambda: found), ((half,),) * 3
-
+        firsts = [depth // GROUPS * i for i in (0, 2, 3)]
+        parts = [weights[i:j] for i, j in zip(firsts, firsts[1:] + [depth])]
+        blocks = Blocks(parts, ((0,), (1,), (2,)), lambda: (firsts, firsts))
+        marks = ((half,),) * 3
+
+    sums = project_early(blocks, 0, inputs, partner)
+    marks = marks[0], (*marks[1], *sums)
     with jax.named_scope("halo"):
         onward = [(i, i + 2) for i in range(1, members - 2, 2)]
         halo = [lax.ppermute(after(x, *mark), "tm", onward) for x, mark in zip(tail, marks)]
 
     tables = (utt_start, stretch_utt, left_stretches)
-    sums = project_early(blocks, inputs, partner)
+    sums = project_early(blocks, 1, inputs, partner, sums)
     with jax.named_scope("halo_first"):
         back = [(i + 1, i) for i in range(0, members, 2)]
         halo_first = [lax.ppermute(after(x, *sums), "tm", back) for x in halo]

time: 74.2 us -> 73.1 us (0.985); the launches traced: 74.4 us -> 72.2 us
  starting transfers between devices: 16.1 us -> 15.1 us
    ppermute x1, starting transfers between devices: 1.08 us -> 0.07 us  [local(): other = lax.ppermute(attended, 'tm', [(i, i ^ 1) for i in range(members)])]
    pallas_call x1, Pallas kernels: 9.07 us -> 8.1 us  [project_late_attend(): pl.pallas_call(functools.partial(late_kernel, blocks), out_shape=[jax.Sha...]
    pallas_call x1 -> x2, Pallas kernels: 7.87 us -> 8.25 us  [project_early(): pl.pallas_call(functools.partial(early_kernel, blocks, step), out_shape=[...]
  transfers between devices with their start and end apart: 15 -> 15, of which waited for: 5 -> 6; matrix products, arithmetic and copies ran while one was open for 0% -> 0% of each run, Pallas kernels for 29% -> 29%
where the time goes in v2:
time: 73.1 us; the launch traced here: 72.2 us
  waiting for transfers between devices  33.1 us (45%)
  Pallas kernels  22.2 us (30%)
  starting transfers between devices  15.1 us (21%)
  local copies, waits for them, and re-layouts  1.42 us (2%)
    ppermute x5, waiting for transfers between devices, along(): lax.ppermute(block, 'dp', [(2 * a + s, 2 * b + s) for a, b in hops for s...  17.1 us
    ppermute x4, waiting for transfers between devices, across(): lax.ppermute(block, 'dp', [(2 * a + s, 2 * a + 1 - s) for a in places for...  16 us
    pallas_call x2, Pallas kernels, project_early(): pl.pallas_call(functools.partial(early_kernel, blocks, step), out_shape=[...  8.25 us
    pallas_call x1, Pallas kernels, project_late_attend(): pl.pallas_call(functools.partial(late_kernel, blocks), out_shape=[jax.Sha...  8.1 us
    ppermute x5, starting transfers between devices, along(): lax.ppermute(block, 'dp', [(2 * a + s, 2 * b + s) for a, b in hops for s...  5.49 us
    ppermute x4, starting transfers between devices, across(): lax.ppermute(block, 'dp', [(2 * a + s, 2 * a + 1 - s) for a in places for...  5.12 us
    pallas_call x1, Pallas kernels, attend_own(): pl.pallas_call(own_kernel, out_shape=jax.ShapeDtypeStruct((rows, width),...  4.01 us
    ppermute x2, starting transfers between devices, local(): halo_first = [lax.ppermute(after(x, *sums), 'tm', back) for x in halo]  2.58 us
  transfers between devices with their start and end apart: 15, of which 6 were waited for; matrix products, arithmetic and copies ran while one was open for 0% of the time, Pallas kernels for 29%

profile of v2, /device:TPU:0, one launch (start us, length us, event | category | flops | bytes accessed | tf_op | source)
XLA Modules:
  0.0 72.2 jit_solution(17788320092582611001)
XLA Ops:
  0.0 0.0 copy-start
  0.0 0.5 collective-permute-start.9
  0.5 1.4 %copy-done.1 = bf16[192,2304]{1,0:T(8,128)(2,1)S(1)} copy-done((bf16[192,2304]{1,0:T(8,128)(2,1)S(1)}, bf16[192,2304]{1,0:T(8,128)(2,1)}, u32[]{:S(2)}) %copy-start.1) | copy-done | bytes 884760
  1.9 0.1 take_half.1.refs_0_
  1.9 2.5 %collective-permute-start = (bf16[192,1152]{1,0:T(8,128)(2,1)S(1)}, bf16[192,1152]{1,0:T(8,128)(2,1)S(1)}, u32[]{:S(2)}, u32[]{:S(2)}) collective-permute-start(bf16[192,1152]{1,0:T(8,128)(2,1)S(1)} %take_half.1.refs_0_), channel_id=1, source_target_pairs={{0,4},{4,0},{8,12},{12,8},{16,20},{20,16},{24,28},{28,24},{1,5},{5... | collective-permute-start | bytes 1327112 | tf_op jit(solution)/shard_map/half_across/ppermute | solution.py:428
  4.5 1.6 %collective-permute-start.1 = (bf16[192,1152]{1,0:T(8,128)(2,1)S(1)}, bf16[192,1152]{1,0:T(8,128)(2,1)S(1)}, u32[]{:S(2)}, u32[]{:S(2)}) collective-permute-start(bf16[192,1152]{1,0:T(8,128)(2,1)S(1)} %take_half.1.refs_0_), channel_id=1, source_target_pairs={{8,0},{12,4},{16,24},{20,28},{0,8},{4,12},{24,16},{28,20},{9,1},{1... | collective-permute-start | bytes 1327112 | tf_op jit(solution)/shard_map/near/ppermute | solution.py:422
  6.1 0.7 collective-permute-start.2
  6.7 8.4 %collective-permute-done.refs_1_ = bf16[192,1152]{1,0:T(8,128)(2,1)S(1)} collective-permute-done((bf16[192,1152]{1,0:T(8,128)(2,1)S(1)}, bf16[192,1152]{1,0:T(8,128)(2,1)S(1)}, u32[]{:S(2)}, u32[]{:S(2)}) %collective-permute-start) | collective-permute-done | bytes 442400 | tf_op jit(solution)/shard_map/half_across/ppermute | solution.py:428
  15.2 1.5 %collective-permute-done.1.refs_2_ = bf16[192,1152]{1,0:T(8,128)(2,1)S(1)} collective-permute-done((bf16[192,1152]{1,0:T(8,128)(2,1)S(1)}, bf16[192,1152]{1,0:T(8,128)(2,1)S(1)}, u32[]{:S(2)}, u32[]{:S(2)}) %collective-permute-start.1) | collective-permute-done | bytes 442400 | tf_op jit(solution)/shard_map/near/ppermute | solution.py:422
  16.6 0.0 collective-permute-done.2.between_ref
  16.6 1.3 %collective-permute-start.4 = (bf16[192,1152]{1,0:T(8,128)(2,1)S(1)}, bf16[192,1152]{1,0:T(8,128)(2,1)S(1)}, u32[]{:S(2)}, u32[]{:S(2)}) collective-permute-start(bf16[192,1152]{1,0:T(8,128)(2,1)S(1)} %collective-permute-done.2.between_ref), channel_id=1, source_target_pairs={{8,0},{12,4},{16,24},{20,28},{9,1},{13,5},{17,25},{21,29},{10,2},{... | collective-permute-start | bytes 1327112 | tf_op jit(solution)/shard_map/end_mid/ppermute | solution.py:422
  17.9 0.4 collective-permute-start.3
  18.3 0.7 collective-permute-start.6
  19.0 13.0 %collective-permute-done.4.end_ref = bf16[192,1152]{1,0:T(8,128)(2,1)S(1)} collective-permute-done((bf16[192,1152]{1,0:T(8,128)(2,1)S(1)}, bf16[192,1152]{1,0:T(8,128)(2,1)S(1)}, u32[]{:S(2)}, u32[]{:S(2)}) %collective-permute-start.4) | collective-permute-done | bytes 442400 | tf_op jit(solution)/shard_map/end_mid/ppermute | solution.py:422
  32.1 0.3 choose.2.refs_0_.refs_4_
  32.3 0.0 collective-permute-done.3.refs_3_
  32.3 0.6 collective-permute-start.5
  32.9 0.0 collective-permute-done.6.between_ref
  32.9 1.3 %collective-permute-start.7 = (bf16[192,1152]{1,0:T(8,128)(2,1)S(1)}, bf16[192,1152]{1,0:T(8,128)(2,1)S(1)}, u32[]{:S(2)}, u32[]{:S(2)}) collective-permute-start(bf16[192,1152]{1,0:T(8,128)(2,1)S(1)} %collective-permute-done.6.between_ref), channel_id=1, source_target_pairs={{8,0},{12,4},{16,24},{20,28},{9,1},{13,5},{17,25},{21,29},{10,2},{... | collective-permute-start | bytes 1327112 | tf_op jit(solution)/shard_map/end_far/ppermute | solution.py:422
  34.2 0.0 copy-done
  34.2 0.1 take_tail.1
  34.4 0.7 collective-permute-start.10
  35.1 0.0 collective-permute-done.9.refs_5_.refs_3_.refs_9_
  35.1 5.2 %project_early.2 = (f32[768,1152]{1,0:T(8,128)S(1)}, f32[768,1152]{1,0:T(8,128)S(1)}) custom-call(bf16[192,1152]{1,0:T(8,128)(2,1)S(1)} %take_half.1.refs_0_, bf16[192,1152]{1,0:T(8,128)(2,1)S(1)} %collective-permute-done.refs_1_, bf16[192,1152]{1,0:T(8,128)(2,1)S(1)} %collective-permute-done.1.refs_2_, ...), custom_call_target="tpu_custom_call" | custom-call | tf_op jit(solution)/shard_map/project_early/pallas_call | solution.py:313
  40.3 2.8 %collective-permute-done.5.refs_1_.refs_5_ = bf16[192,1152]{1,0:T(8,128)(2,1)S(1)} collective-permute-done((bf16[192,1152]{1,0:T(8,128)(2,1)S(1)}, bf16[192,1152]{1,0:T(8,128)(2,1)S(1)}, u32[]{:S(2)}, u32[]{:S(2)}) %collective-permute-start.5) | collective-permute-done | bytes 442400 | tf_op jit(solution)/shard_map/second_across/ppermute | solution.py:428
  43.1 2.6 %collective-permute-done.7.end_ref = bf16[192,1152]{1,0:T(8,128)(2,1)S(1)} collective-permute-done((bf16[192,1152]{1,0:T(8,128)(2,1)S(1)}, bf16[192,1152]{1,0:T(8,128)(2,1)S(1)}, u32[]{:S(2)}, u32[]{:S(2)}) %collective-permute-start.7) | collective-permute-done | bytes 442400 | tf_op jit(solution)/shard_map/end_far/ppermute | solution.py:422
  45.7 0.7 collective-permute-start.11
  46.4 0.3 choose.3.refs_6_
  46.7 0.0 copy-start.2
  46.7 0.0 copy-start.3
  46.7 0.0 copy-start.4
  46.7 1.6 %collective-permute-start.8 = (bf16[192,1152]{1,0:T(8,128)(2,1)S(1)}, bf16[192,1152]{1,0:T(8,128)(2,1)S(1)}, u32[]{:S(2)}, u32[]{:S(2)}) collective-permute-start(bf16[192,1152]{1,0:T(8,128)(2,1)S(1)} %choose.3.refs_6_), channel_id=1, source_target_pairs={{0,4},{4,0},{8,12},{12,8},{16,20},{20,16},{24,28},{28,24},{1,5},{5... | collective-permute-start | bytes 1327112 | tf_op jit(solution)/shard_map/third_across/ppermute | solution.py:428
  48.3 3.0 %project_early.3 = (f32[768,1152]{1,0:T(8,128)S(1)}, f32[768,1152]{1,0:T(8,128)S(1)}) custom-call(bf16[192,1152]{1,0:T(8,128)(2,1)S(1)} %choose.2.refs_0_.refs_4_, bf16[192,1152]{1,0:T(8,128)(2,1)S(1)} %collective-permute-done.5.refs_1_.refs_5_, bf16[768,1536]{1,0:T(8,128)(2,1)S(1)} %bitcast.5, ...), custom_call_target="tpu_custom_call" | custom-call | tf_op jit(solution)/shard_map/project_early/pallas_call | solution.py:313
  51.3 0.0 collective-permute-done.10.refs_10_
  51.3 1.3 %collective-permute-start.12 = (bf16[256,1536]{1,0:T(8,128)(2,1)S(1)}, bf16[256,1536]{1,0:T(8,128)(2,1)S(1)}, u32[]{:S(2)}, u32[]{:S(2)}) collective-permute-start(bf16[256,1536]{1,0:T(8,128)(2,1)S(1)} %collective-permute-done.10.refs_10_), channel_id=1, source_target_pairs={{1,0},{3,2},{5,4},{7,6},{9,8},{11,10},{13,12},{15,14},{17,16},{19,... | collective-permute-start | bytes 2359304 | tf_op jit(solution)/shard_map/halo_first/ppermute | solution.py:500
  52.6 0.0 collective-permute-done.11.refs_11_
  52.6 1.3 %collective-permute-start.13 = (bf16[256,1536]{1,0:T(8,128)(2,1)S(1)}, bf16[256,1536]{1,0:T(8,128)(2,1)S(1)}, u32[]{:S(2)}, u32[]{:S(2)}) collective-permute-start(bf16[256,1536]{1,0:T(8,128)(2,1)S(1)} %collective-permute-done.11.refs_11_), channel_id=1, source_target_pairs={{1,0},{3,2},{5,4},{7,6},{9,8},{11,10},{13,12},{15,14},{17,16},{19,... | collective-permute-start | bytes 2359304 | tf_op jit(solution)/shard_map/halo_first/ppermute | solution.py:500
  53.9 4.7 %collective-permute-done.8.refs_7_ = bf16[192,1152]{1,0:T(8,128)(2,1)S(1)} collective-permute-done((bf16[192,1152]{1,0:T(8,128)(2,1)S(1)}, bf16[192,1152]{1,0:T(8,128)(2,1)S(1)}, u32[]{:S(2)}, u32[]{:S(2)}) %collective-permute-start.8) | collective-permute-done | bytes 442400 | tf_op jit(solution)/shard_map/third_across/ppermute | solution.py:428
  58.7 0.0 copy-done.2
  58.7 0.0 copy-done.3
  58.7 0.0 copy-done.4
  58.7 8.1 %project_late_attend.1 = (bf16[1024,384]{1,0:T(8,128)(2,1)S(1)}, bf16[1536,384]{1,0:T(8,128)(2,1)S(1)}, bf16[2048,384]{1,0:T(8,128)(2,1)S(1)}, bf16[2048,384]{1,0:T(8,128)(2,1)S(1)}, bf16[1536,768]{1,0:T(8,128)(2,1)S(1)}) custom-call(s32[1,3]{1,0:T(1,128)S(1)} %copy-done.2, s32[1,12]{1,0:T(1,128)S(1)} %copy-done.3, s32[1,12]{1,0:T(1,128)S(1)} %copy-done.4, ...), custom_call_target="tpu_custom_call" | custom-call | tf_op jit(solution)/shard_map/project_late_attend/pallas_call | solution.py:359
  66.8 0.1 collective-permute-start.14
  66.9 0.0 collective-permute-done.12.refs_0_
  66.9 0.0 collective-permute-done.13.refs_1_
  66.9 4.0 %attend_own.1.own_ref = bf16[768,384]{1,0:T(8,128)(2,1)S(1)} custom-call(s32[1,3]{1,0:T(1,128)S(1)} %copy-done.2, s32[1,12]{1,0:T(1,128)S(1)} %copy-done.3, s32[1,12]{1,0:T(1,128)S(1)} %copy-done.4, bf16[1536,384]{1,0:T(8,128)(2,1)S(1)} %get-tuple-element.38.q_ref, bf16[2048,384]{1,0:T(8,128)(2,1)S(1)} %get-tuple-element.39.k_ref, ...), custom_call_target="tpu_custom_call" | custom-call | tf_op jit(solution)/shard_map/attend_own/pallas_call | solution.py:384
  70.9 0.0 collective-permute-done.14.other_ref
  71.0 1.0 %join.1 = bf16[768,768]{1,0:T(8,128)(2,1)} custom-call(bf16[768,384]{1,0:T(8,128)(2,1)S(1)} %attend_own.1.own_ref, bf16[1024,384]{1,0:T(8,128)(2,1)S(1)} %collective-permute-done.14.other_ref), custom_call_target="tpu_custom_call" | custom-call | tf_op jit(solution)/shard_map/join/pallas_call | solution.py:297
  (1 shorter events, 0.0 us)
Async XLA Ops:
  0.0 34.2 %copy-start = (bf16[1,768,1536]{2,1,0:T(8,128)(2,1)S(1)}, bf16[1,768,1536]{2,1,0:T(8,128)(2,1)}, u32[]{:S(2)}) copy-start(bf16[1,768,1536]{2,1,0:T(8,128)(2,1)} %param.5) | copy-start | bytes 7077892
  0.0 35.1 %collective-permute-start.9 = (bf16[768,1536]{1,0:T(8,128)(2,1)}, bf16[768,1536]{1,0:T(8,128)(2,1)S(1)}, u32[]{:S(2)}, u32[]{:S(2)}) collective-permute-start(bf16[768,1536]{1,0:T(8,128)(2,1)} %bitcast.2), channel_id=1, source_target_pairs={{0,1},{1,0},{2,3},{3,2},{4,5},{5,4},{6,7},{7,6},{8,9},{9,8},{10,11... | collective-permute-start | bytes 7077896 | tf_op jit(solution)/shard_map/partner/ppermute | solution.py:480
  0.5 1.4 %copy-start.1 = (bf16[192,2304]{1,0:T(8,128)(2,1)S(1)}, bf16[192,2304]{1,0:T(8,128)(2,1)}, u32[]{:S(2)}) copy-start(bf16[192,2304]{1,0:T(8,128)(2,1)} %w_ref.1) | copy-start | bytes 2654212
  1.9 13.2 %collective-permute-start = (bf16[192,1152]{1,0:T(8,128)(2,1)S(1)}, bf16[192,1152]{1,0:T(8,128)(2,1)S(1)}, u32[]{:S(2)}, u32[]{:S(2)}) collective-permute-start(bf16[192,1152]{1,0:T(8,128)(2,1)S(1)} %take_half.1.refs_0_), channel_id=1, source_target_pairs={{0,4},{4,0},{8,12},{12,8},{16,20},{20,16},{24,28},{28,24},{1,5},{5... | collective-permute-start | bytes 1327112 | tf_op jit(solution)/shard_map/half_across/ppermute | solution.py:428
  4.5 12.2 %collective-permute-start.1 = (bf16[192,1152]{1,0:T(8,128)(2,1)S(1)}, bf16[192,1152]{1,0:T(8,128)(2,1)S(1)}, u32[]{:S(2)}, u32[]{:S(2)}) collective-permute-start(bf16[192,1152]{1,0:T(8,128)(2,1)S(1)} %take_half.1.refs_0_), channel_id=1, source_target_pairs={{8,0},{12,4},{16,24},{20,28},{0,8},{4,12},{24,16},{28,20},{9,1},{1... | collective-permute-start | bytes 1327112 | tf_op jit(solution)/shard_map/near/ppermute | solution.py:422
  6.1 10.6 %collective-permute-start.2 = (bf16[192,1152]{1,0:T(8,128)(2,1)S(1)}, bf16[192,1152]{1,0:T(8,128)(2,1)S(1)}, u32[]{:S(2)}, u32[]{:S(2)}) collective-permute-start(bf16[192,1152]{1,0:T(8,128)(2,1)S(1)} %take_half.1.refs_0_), channel_id=1, source_target_pairs={{8,16},{12,20},{16,8},{20,12},{9,17},{13,21},{17,9},{21,13},{10,18... | collective-permute-start | bytes 1327112 | tf_op jit(solution)/shard_map/mid/ppermute | solution.py:422
  16.6 15.4 %collective-permute-start.4 = (bf16[192,1152]{1,0:T(8,128)(2,1)S(1)}, bf16[192,1152]{1,0:T(8,128)(2,1)S(1)}, u32[]{:S(2)}, u32[]{:S(2)}) collective-permute-start(bf16[192,1152]{1,0:T(8,128)(2,1)S(1)} %collective-permute-done.2.between_ref), channel_id=1, source_target_pairs={{8,0},{12,4},{16,24},{20,28},{9,1},{13,5},{17,25},{21,29},{10,2},{... | collective-permute-start | bytes 1327112 | tf_op jit(solution)/shard_map/end_mid/ppermute | solution.py:422
  17.9 14.4 %collective-permute-start.3 = (bf16[192,1152]{1,0:T(8,128)(2,1)S(1)}, bf16[192,1152]{1,0:T(8,128)(2,1)S(1)}, u32[]{:S(2)}, u32[]{:S(2)}) collective-permute-start(bf16[192,1152]{1,0:T(8,128)(2,1)S(1)} %collective-permute-done.1.refs_2_), channel_id=1, source_target_pairs={{0,4},{4,0},{8,12},{12,8},{16,20},{20,16},{24,28},{28,24},{1,5},{5... | collective-permute-start | bytes 1327112 | tf_op jit(solution)/shard_map/near_across/ppermute | solution.py:428
  18.3 14.6 %collective-permute-start.6 = (bf16[192,1152]{1,0:T(8,128)(2,1)S(1)}, bf16[192,1152]{1,0:T(8,128)(2,1)S(1)}, u32[]{:S(2)}, u32[]{:S(2)}) collective-permute-start(bf16[192,1152]{1,0:T(8,128)(2,1)S(1)} %collective-permute-done.1.refs_2_), channel_id=1, source_target_pairs={{8,16},{12,20},{16,8},{20,12},{9,17},{13,21},{17,9},{21,13},{10,18... | collective-permute-start | bytes 1327112 | tf_op jit(solution)/shard_map/mid_far/ppermute | solution.py:422
  32.3 10.7 %collective-permute-start.5 = (bf16[192,1152]{1,0:T(8,128)(2,1)S(1)}, bf16[192,1152]{1,0:T(8,128)(2,1)S(1)}, u32[]{:S(2)}, u32[]{:S(2)}) collective-permute-start(bf16[192,1152]{1,0:T(8,128)(2,1)S(1)} %choose.2.refs_0_.refs_4_), channel_id=1, source_target_pairs={{0,4},{4,0},{8,12},{12,8},{16,20},{20,16},{24,28},{28,24},{1,5},{5... | collective-permute-start | bytes 1327112 | tf_op jit(solution)/shard_map/second_across/ppermute | solution.py:428
  32.9 12.8 %collective-permute-start.7 = (bf16[192,1152]{1,0:T(8,128)(2,1)S(1)}, bf16[192,1152]{1,0:T(8,128)(2,1)S(1)}, u32[]{:S(2)}, u32[]{:S(2)}) collective-permute-start(bf16[192,1152]{1,0:T(8,128)(2,1)S(1)} %collective-permute-done.6.between_ref), channel_id=1, source_target_pairs={{8,0},{12,4},{16,24},{20,28},{9,1},{13,5},{17,25},{21,29},{10,2},{... | collective-permute-start | bytes 1327112 | tf_op jit(solution)/shard_map/end_far/ppermute | solution.py:422
  34.4 17.0 %collective-permute-start.10 = (bf16[256,1536]{1,0:T(8,128)(2,1)S(1)}, bf16[256,1536]{1,0:T(8,128)(2,1)S(1)}, u32[]{:S(2)}, u32[]{:S(2)}) collective-permute-start(bf16[256,1536]{1,0:T(8,128)(2,1)S(1)} %get-tuple-element.31), channel_id=1, source_target_pairs={{1,3},{5,7},{9,11},{13,15},{17,19},{21,23},{25,27},{29,31}} | collective-permute-start | bytes 2359304 | tf_op jit(solution)/shard_map/halo/ppermute | solution.py:494
  45.7 7.0 %collective-permute-start.11 = (bf16[256,1536]{1,0:T(8,128)(2,1)S(1)}, bf16[256,1536]{1,0:T(8,128)(2,1)S(1)}, u32[]{:S(2)}, u32[]{:S(2)}) collective-permute-start(bf16[256,1536]{1,0:T(8,128)(2,1)S(1)} %get-tuple-element.35), channel_id=1, source_target_pairs={{1,3},{5,7},{9,11},{13,15},{17,19},{21,23},{25,27},{29,31}} | collective-permute-start | bytes 2359304 | tf_op jit(solution)/shard_map/halo/ppermute | solution.py:494
  46.7 12.0 %copy-start.2 = (s32[1,3]{1,0:T(1,128)S(1)}, s32[1,3]{1,0:T(1,128)}, u32[]{:S(2)}) copy-start(s32[1,3]{1,0:T(1,128)} %start_ref.3) | copy-start | bytes 40
  46.7 12.0 %copy-start.3 = (s32[1,12]{1,0:T(1,128)S(1)}, s32[1,12]{1,0:T(1,128)}, u32[]{:S(2)}) copy-start(s32[1,12]{1,0:T(1,128)} %owner_ref.3) | copy-start | bytes 148
  46.7 12.0 %copy-start.4 = (s32[1,12]{1,0:T(1,128)S(1)}, s32[1,12]{1,0:T(1,128)}, u32[]{:S(2)}) copy-start(s32[1,12]{1,0:T(1,128)} %left_ref.3) | copy-start | bytes 148
  46.7 12.0 %collective-permute-start.8 = (bf16[192,1152]{1,0:T(8,128)(2,1)S(1)}, bf16[192,1152]{1,0:T(8,128)(2,1)S(1)}, u32[]{:S(2)}, u32[]{:S(2)}) collective-permute-start(bf16[192,1152]{1,0:T(8,128)(2,1)S(1)} %choose.3.refs_6_), channel_id=1, source_target_pairs={{0,4},{4,0},{8,12},{12,8},{16,20},{20,16},{24,28},{28,24},{1,5},{5... | collective-permute-start | bytes 1327112 | tf_op jit(solution)/shard_map/third_across/ppermute | solution.py:428
  51.3 15.6 %collective-permute-start.12 = (bf16[256,1536]{1,0:T(8,128)(2,1)S(1)}, bf16[256,1536]{1,0:T(8,128)(2,1)S(1)}, u32[]{:S(2)}, u32[]{:S(2)}) collective-permute-start(bf16[256,1536]{1,0:T(8,128)(2,1)S(1)} %collective-permute-done.10.refs_10_), channel_id=1, source_target_pairs={{1,0},{3,2},{5,4},{7,6},{9,8},{11,10},{13,12},{15,14},{17,16},{19,... | collective-permute-start | bytes 2359304 | tf_op jit(solution)/shard_map/halo_first/ppermute | solution.py:500
  52.6 14.3 %collective-permute-start.13 = (bf16[256,1536]{1,0:T(8,128)(2,1)S(1)}, bf16[256,1536]{1,0:T(8,128)(2,1)S(1)}, u32[]{:S(2)}, u32[]{:S(2)}) collective-permute-start(bf16[256,1536]{1,0:T(8,128)(2,1)S(1)} %collective-permute-done.11.refs_11_), channel_id=1, source_target_pairs={{1,0},{3,2},{5,4},{7,6},{9,8},{11,10},{13,12},{15,14},{17,16},{19,... | collective-permute-start | bytes 2359304 | tf_op jit(solution)/shard_map/halo_first/ppermute | solution.py:500
  66.8 4.1 %collective-permute-start.14 = (bf16[1024,384]{1,0:T(8,128)(2,1)S(1)}, bf16[1024,384]{1,0:T(8,128)(2,1)S(1)}, u32[]{:S(2)}, u32[]{:S(2)}) collective-permute-start(bf16[1024,384]{1,0:T(8,128)(2,1)S(1)} %get-tuple-element.44.refs_2_), channel_id=1, source_target_pairs={{0,1},{1,0},{2,3},{3,2},{4,5},{5,4},{6,7},{7,6},{8,9},{9,8},{10,11... | collective-permute-start | bytes 2359304 | tf_op jit(solution)/shard_map/swap/ppermute | solution.py:505

commit v3 on v2

--- a/solution.py
+++ b/solution.py
@@ -464,7 +464,7 @@
         third,
         third_across,
     ]
-    marks = (near_across, mid_far, end_mid), (second_across, end_far), (third_across,)
+    marks = (near_across, mid_far, end_mid), (second_across,), (third_across,)
     return Blocks(blocks, ((0, 1, 2, 3), (4, 5), (6, 7)), find), marks
 
 

time: 73.1 us -> 71.1 us (0.973)
  waiting for transfers between devices: 33.1 us -> 30.8 us
    ppermute x4, waiting for transfers between devices: 16 us -> 14.4 us  [across(): lax.ppermute(block, 'dp', [(2 * a + s, 2 * a + 1 - s) for a in places for...]
  transfers between devices with their start and end apart: 15 -> 15, of which waited for: 6 -> 6; matrix products, arithmetic and copies ran while one was open for 0% -> 0% of each run, Pallas kernels for 29% -> 30%
where the time goes in v3:
time: 71.1 us; the launch traced here: 69.9 us
  waiting for transfers between devices  30.8 us (43%)
  Pallas kernels  22.1 us (31%)
  starting transfers between devices  15.1 us (21%)
  local copies, waits for them, and re-layouts  1.42 us (2%)
    ppermute x5, waiting for transfers between devices, along(): lax.ppermute(block, 'dp', [(2 * a + s, 2 * b + s) for a, b in hops for s...  16.4 us
    ppermute x4, waiting for transfers between devices, across(): lax.ppermute(block, 'dp', [(2 * a + s, 2 * a + 1 - s) for a in places for...  14.4 us
    pallas_call x1, Pallas kernels, project_late_attend(): pl.pallas_call(functools.partial(late_kernel, blocks), out_shape=[jax.Sha...  8.49 us
    pallas_call x2, Pallas kernels, project_early(): pl.pallas_call(functools.partial(early_kernel, blocks, step), out_shape=[...  8.25 us
    ppermute x5, starting transfers between devices, along(): lax.ppermute(block, 'dp', [(2 * a + s, 2 * b + s) for a, b in hops for s...  5.49 us
    ppermute x4, starting transfers between devices, across(): lax.ppermute(block, 'dp', [(2 * a + s, 2 * a + 1 - s) for a in places for...  5.12 us
    pallas_call x1, Pallas kernels, attend_own(): pl.pallas_call(own_kernel, out_shape=jax.ShapeDtypeStruct((rows, width),...  3.62 us
    ppermute x2, starting transfers between devices, local(): halo_first = [lax.ppermute(after(x, *sums), 'tm', back) for x in halo]  2.58 us
  transfers between devices with their start and end apart: 15, of which 6 were waited for; matrix products, arithmetic and copies ran while one was open for 0% of the time, Pallas kernels for 30%

profile of v3, /device:TPU:0, one launch (start us, length us, event | category | flops | bytes accessed | tf_op | source)
XLA Modules:
  0.0 69.9 jit_solution(9835515806193696115)
XLA Ops:
  0.0 0.0 copy-start
  0.0 0.5 collective-permute-start.9
  0.5 1.4 %copy-done.1 = bf16[192,2304]{1,0:T(8,128)(2,1)S(1)} copy-done((bf16[192,2304]{1,0:T(8,128)(2,1)S(1)}, bf16[192,2304]{1,0:T(8,128)(2,1)}, u32[]{:S(2)}) %copy-start.1) | copy-done | bytes 884760
  1.9 0.1 take_half.1.refs_0_
  1.9 2.5 %collective-permute-start = (bf16[192,1152]{1,0:T(8,128)(2,1)S(1)}, bf16[192,1152]{1,0:T(8,128)(2,1)S(1)}, u32[]{:S(2)}, u32[]{:S(2)}) collective-permute-start(bf16[192,1152]{1,0:T(8,128)(2,1)S(1)} %take_half.1.refs_0_), channel_id=1, source_target_pairs={{0,4},{4,0},{8,12},{12,8},{16,20},{20,16},{24,28},{28,24},{1,5},{5... | collective-permute-start | bytes 1327112 | tf_op jit(solution)/shard_map/half_across/ppermute | solution.py:428
  4.5 1.6 %collective-permute-start.1 = (bf16[192,1152]{1,0:T(8,128)(2,1)S(1)}, bf16[192,1152]{1,0:T(8,128)(2,1)S(1)}, u32[]{:S(2)}, u32[]{:S(2)}) collective-permute-start(bf16[192,1152]{1,0:T(8,128)(2,1)S(1)} %take_half.1.refs_0_), channel_id=1, source_target_pairs={{8,0},{12,4},{16,24},{20,28},{0,8},{4,12},{24,16},{28,20},{9,1},{1... | collective-permute-start | bytes 1327112 | tf_op jit(solution)/shard_map/near/ppermute | solution.py:422
  6.1 0.7 collective-permute-start.2
  6.7 8.4 %collective-permute-done.refs_1_ = bf16[192,1152]{1,0:T(8,128)(2,1)S(1)} collective-permute-done((bf16[192,1152]{1,0:T(8,128)(2,1)S(1)}, bf16[192,1152]{1,0:T(8,128)(2,1)S(1)}, u32[]{:S(2)}, u32[]{:S(2)}) %collective-permute-start) | collective-permute-done | bytes 442400 | tf_op jit(solution)/shard_map/half_across/ppermute | solution.py:428
  15.2 1.5 %collective-permute-done.1.refs_2_ = bf16[192,1152]{1,0:T(8,128)(2,1)S(1)} collective-permute-done((bf16[192,1152]{1,0:T(8,128)(2,1)S(1)}, bf16[192,1152]{1,0:T(8,128)(2,1)S(1)}, u32[]{:S(2)}, u32[]{:S(2)}) %collective-permute-start.1) | collective-permute-done | bytes 442400 | tf_op jit(solution)/shard_map/near/ppermute | solution.py:422
  16.6 0.0 collective-permute-done.2.between_ref
  16.6 1.3 %collective-permute-start.4 = (bf16[192,1152]{1,0:T(8,128)(2,1)S(1)}, bf16[192,1152]{1,0:T(8,128)(2,1)S(1)}, u32[]{:S(2)}, u32[]{:S(2)}) collective-permute-start(bf16[192,1152]{1,0:T(8,128)(2,1)S(1)} %collective-permute-done.2.between_ref), channel_id=1, source_target_pairs={{8,0},{12,4},{16,24},{20,28},{9,1},{13,5},{17,25},{21,29},{10,2},{... | collective-permute-start | bytes 1327112 | tf_op jit(solution)/shard_map/end_mid/ppermute | solution.py:422
  17.9 0.4 collective-permute-start.3
  18.3 0.7 collective-permute-start.6
  19.0 13.0 %collective-permute-done.4.end_ref = bf16[192,1152]{1,0:T(8,128)(2,1)S(1)} collective-permute-done((bf16[192,1152]{1,0:T(8,128)(2,1)S(1)}, bf16[192,1152]{1,0:T(8,128)(2,1)S(1)}, u32[]{:S(2)}, u32[]{:S(2)}) %collective-permute-start.4) | collective-permute-done | bytes 442400 | tf_op jit(solution)/shard_map/end_mid/ppermute | solution.py:422
  32.1 0.3 choose.2.refs_0_.refs_4_
  32.3 0.0 collective-permute-done.3.refs_3_
  32.3 0.6 collective-permute-start.5
  32.9 0.0 collective-permute-done.6.between_ref
  32.9 1.3 %collective-permute-start.7 = (bf16[192,1152]{1,0:T(8,128)(2,1)S(1)}, bf16[192,1152]{1,0:T(8,128)(2,1)S(1)}, u32[]{:S(2)}, u32[]{:S(2)}) collective-permute-start(bf16[192,1152]{1,0:T(8,128)(2,1)S(1)} %collective-permute-done.6.between_ref), channel_id=1, source_target_pairs={{8,0},{12,4},{16,24},{20,28},{9,1},{13,5},{17,25},{21,29},{10,2},{... | collective-permute-start | bytes 1327112 | tf_op jit(solution)/shard_map/end_far/ppermute | solution.py:422
  34.2 0.0 copy-done
  34.2 0.1 take_tail.1
  34.4 0.7 %collective-permute-start.10 = (bf16[256,1536]{1,0:T(8,128)(2,1)S(1)}, bf16[256,1536]{1,0:T(8,128)(2,1)S(1)}, u32[]{:S(2)}, u32[]{:S(2)}) collective-permute-start(bf16[256,1536]{1,0:T(8,128)(2,1)S(1)} %get-tuple-element.31), channel_id=1, source_target_pairs={{1,3},{5,7},{9,11},{13,15},{17,19},{21,23},{25,27},{29,31}} | collective-permute-start | bytes 2359304 | tf_op jit(solution)/shard_map/halo/ppermute | solution.py:494
  35.1 0.0 collective-permute-done.9.refs_5_.refs_3_.refs_9_
  35.1 5.2 %project_early.2 = (f32[768,1152]{1,0:T(8,128)S(1)}, f32[768,1152]{1,0:T(8,128)S(1)}) custom-call(bf16[192,1152]{1,0:T(8,128)(2,1)S(1)} %take_half.1.refs_0_, bf16[192,1152]{1,0:T(8,128)(2,1)S(1)} %collective-permute-done.refs_1_, bf16[192,1152]{1,0:T(8,128)(2,1)S(1)} %collective-permute-done.1.refs_2_, ...), custom_call_target="tpu_custom_call" | custom-call | tf_op jit(solution)/shard_map/project_early/pallas_call | solution.py:313
  40.3 2.8 %collective-permute-done.5.refs_1_.refs_5_ = bf16[192,1152]{1,0:T(8,128)(2,1)S(1)} collective-permute-done((bf16[192,1152]{1,0:T(8,128)(2,1)S(1)}, bf16[192,1152]{1,0:T(8,128)(2,1)S(1)}, u32[]{:S(2)}, u32[]{:S(2)}) %collective-permute-start.5) | collective-permute-done | bytes 442400 | tf_op jit(solution)/shard_map/second_across/ppermute | solution.py:428
  43.1 0.7 %collective-permute-start.11 = (bf16[256,1536]{1,0:T(8,128)(2,1)S(1)}, bf16[256,1536]{1,0:T(8,128)(2,1)S(1)}, u32[]{:S(2)}, u32[]{:S(2)}) collective-permute-start(bf16[256,1536]{1,0:T(8,128)(2,1)S(1)} %get-tuple-element.35), channel_id=1, source_target_pairs={{1,3},{5,7},{9,11},{13,15},{17,19},{21,23},{25,27},{29,31}} | collective-permute-start | bytes 2359304 | tf_op jit(solution)/shard_map/halo/ppermute | solution.py:494
  43.8 1.9 %collective-permute-done.7.end_ref = bf16[192,1152]{1,0:T(8,128)(2,1)S(1)} collective-permute-done((bf16[192,1152]{1,0:T(8,128)(2,1)S(1)}, bf16[192,1152]{1,0:T(8,128)(2,1)S(1)}, u32[]{:S(2)}, u32[]{:S(2)}) %collective-permute-start.7) | collective-permute-done | bytes 442400 | tf_op jit(solution)/shard_map/end_far/ppermute | solution.py:422
  45.7 0.3 choose.3.refs_6_
  45.9 0.0 copy-start.2
  45.9 0.0 copy-start.3
  46.0 0.0 copy-start.4
  46.0 1.6 %collective-permute-start.8 = (bf16[192,1152]{1,0:T(8,128)(2,1)S(1)}, bf16[192,1152]{1,0:T(8,128)(2,1)S(1)}, u32[]{:S(2)}, u32[]{:S(2)}) collective-permute-start(bf16[192,1152]{1,0:T(8,128)(2,1)S(1)} %choose.3.refs_6_), channel_id=1, source_target_pairs={{0,4},{4,0},{8,12},{12,8},{16,20},{20,16},{24,28},{28,24},{1,5},{5... | collective-permute-start | bytes 1327112 | tf_op jit(solution)/shard_map/third_across/ppermute | solution.py:428
  47.6 3.0 %project_early.3 = (f32[768,1152]{1,0:T(8,128)S(1)}, f32[768,1152]{1,0:T(8,128)S(1)}) custom-call(bf16[192,1152]{1,0:T(8,128)(2,1)S(1)} %choose.2.refs_0_.refs_4_, bf16[192,1152]{1,0:T(8,128)(2,1)S(1)} %collective-permute-done.5.refs_1_.refs_5_, bf16[768,1536]{1,0:T(8,128)(2,1)S(1)} %bitcast.5, ...), custom_call_target="tpu_custom_call" | custom-call | tf_op jit(solution)/shard_map/project_early/pallas_call | solution.py:313
  50.6 0.0 collective-permute-done.10.refs_10_
  50.6 1.3 %collective-permute-start.12 = (bf16[256,1536]{1,0:T(8,128)(2,1)S(1)}, bf16[256,1536]{1,0:T(8,128)(2,1)S(1)}, u32[]{:S(2)}, u32[]{:S(2)}) collective-permute-start(bf16[256,1536]{1,0:T(8,128)(2,1)S(1)} %collective-permute-done.10.refs_10_), channel_id=1, source_target_pairs={{1,0},{3,2},{5,4},{7,6},{9,8},{11,10},{13,12},{15,14},{17,16},{19,... | collective-permute-start | bytes 2359304 | tf_op jit(solution)/shard_map/halo_first/ppermute | solution.py:500
  51.9 0.0 collective-permute-done.11.refs_11_
  51.9 1.3 %collective-permute-start.13 = (bf16[256,1536]{1,0:T(8,128)(2,1)S(1)}, bf16[256,1536]{1,0:T(8,128)(2,1)S(1)}, u32[]{:S(2)}, u32[]{:S(2)}) collective-permute-start(bf16[256,1536]{1,0:T(8,128)(2,1)S(1)} %collective-permute-done.11.refs_11_), channel_id=1, source_target_pairs={{1,0},{3,2},{5,4},{7,6},{9,8},{11,10},{13,12},{15,14},{17,16},{19,... | collective-permute-start | bytes 2359304 | tf_op jit(solution)/shard_map/halo_first/ppermute | solution.py:500
  53.2 3.2 %collective-permute-done.8.refs_7_ = bf16[192,1152]{1,0:T(8,128)(2,1)S(1)} collective-permute-done((bf16[192,1152]{1,0:T(8,128)(2,1)S(1)}, bf16[192,1152]{1,0:T(8,128)(2,1)S(1)}, u32[]{:S(2)}, u32[]{:S(2)}) %collective-permute-start.8) | collective-permute-done | bytes 442400 | tf_op jit(solution)/shard_map/third_across/ppermute | solution.py:428
  56.4 0.0 copy-done.2
  56.4 0.0 copy-done.3
  56.4 0.0 copy-done.4
  56.4 8.5 %project_late_attend.1 = (bf16[1024,384]{1,0:T(8,128)(2,1)S(1)}, bf16[1536,384]{1,0:T(8,128)(2,1)S(1)}, bf16[2048,384]{1,0:T(8,128)(2,1)S(1)}, bf16[2048,384]{1,0:T(8,128)(2,1)S(1)}, bf16[1536,768]{1,0:T(8,128)(2,1)S(1)}) custom-call(s32[1,3]{1,0:T(1,128)S(1)} %copy-done.2, s32[1,12]{1,0:T(1,128)S(1)} %copy-done.3, s32[1,12]{1,0:T(1,128)S(1)} %copy-done.4, ...), custom_call_target="tpu_custom_call" | custom-call | tf_op jit(solution)/shard_map/project_late_attend/pallas_call | solution.py:359
  64.9 0.1 collective-permute-start.14
  65.0 0.0 collective-permute-done.12.refs_0_
  65.0 0.0 collective-permute-done.13.refs_1_
  65.0 3.6 %attend_own.1.own_ref = bf16[768,384]{1,0:T(8,128)(2,1)S(1)} custom-call(s32[1,3]{1,0:T(1,128)S(1)} %copy-done.2, s32[1,12]{1,0:T(1,128)S(1)} %copy-done.3, s32[1,12]{1,0:T(1,128)S(1)} %copy-done.4, bf16[1536,384]{1,0:T(8,128)(2,1)S(1)} %get-tuple-element.38.q_ref, bf16[2048,384]{1,0:T(8,128)(2,1)S(1)} %get-tuple-element.39.k_ref, ...), custom_call_target="tpu_custom_call" | custom-call | tf_op jit(solution)/shard_map/attend_own/pallas_call | solution.py:384
  68.6 0.0 collective-permute-done.14.other_ref
  68.7 1.0 %join.1 = bf16[768,768]{1,0:T(8,128)(2,1)} custom-call(bf16[768,384]{1,0:T(8,128)(2,1)S(1)} %attend_own.1.own_ref, bf16[1024,384]{1,0:T(8,128)(2,1)S(1)} %collective-permute-done.14.other_ref), custom_call_target="tpu_custom_call" | custom-call | tf_op jit(solution)/shard_map/join/pallas_call | solution.py:297
  (1 shorter events, 0.0 us)
Async XLA Ops:
  0.0 34.2 %copy-start = (bf16[1,768,1536]{2,1,0:T(8,128)(2,1)S(1)}, bf16[1,768,1536]{2,1,0:T(8,128)(2,1)}, u32[]{:S(2)}) copy-start(bf16[1,768,1536]{2,1,0:T(8,128)(2,1)} %param.5) | copy-start | bytes 7077892
  0.0 35.1 %collective-permute-start.9 = (bf16[768,1536]{1,0:T(8,128)(2,1)}, bf16[768,1536]{1,0:T(8,128)(2,1)S(1)}, u32[]{:S(2)}, u32[]{:S(2)}) collective-permute-start(bf16[768,1536]{1,0:T(8,128)(2,1)} %bitcast.2), channel_id=1, source_target_pairs={{0,1},{1,0},{2,3},{3,2},{4,5},{5,4},{6,7},{7,6},{8,9},{9,8},{10,11... | collective-permute-start | bytes 7077896 | tf_op jit(solution)/shard_map/partner/ppermute | solution.py:480
  0.5 1.4 %copy-start.1 = (bf16[192,2304]{1,0:T(8,128)(2,1)S(1)}, bf16[192,2304]{1,0:T(8,128)(2,1)}, u32[]{:S(2)}) copy-start(bf16[192,2304]{1,0:T(8,128)(2,1)} %w_ref.1) | copy-start | bytes 2654212
  1.9 13.2 %collective-permute-start = (bf16[192,1152]{1,0:T(8,128)(2,1)S(1)}, bf16[192,1152]{1,0:T(8,128)(2,1)S(1)}, u32[]{:S(2)}, u32[]{:S(2)}) collective-permute-start(bf16[192,1152]{1,0:T(8,128)(2,1)S(1)} %take_half.1.refs_0_), channel_id=1, source_target_pairs={{0,4},{4,0},{8,12},{12,8},{16,20},{20,16},{24,28},{28,24},{1,5},{5... | collective-permute-start | bytes 1327112 | tf_op jit(solution)/shard_map/half_across/ppermute | solution.py:428
  4.5 12.2 %collective-permute-start.1 = (bf16[192,1152]{1,0:T(8,128)(2,1)S(1)}, bf16[192,1152]{1,0:T(8,128)(2,1)S(1)}, u32[]{:S(2)}, u32[]{:S(2)}) collective-permute-start(bf16[192,1152]{1,0:T(8,128)(2,1)S(1)} %take_half.1.refs_0_), channel_id=1, source_target_pairs={{8,0},{12,4},{16,24},{20,28},{0,8},{4,12},{24,16},{28,20},{9,1},{1... | collective-permute-start | bytes 1327112 | tf_op jit(solution)/shard_map/near/ppermute | solution.py:422
  6.1 10.6 %collective-permute-start.2 = (bf16[192,1152]{1,0:T(8,128)(2,1)S(1)}, bf16[192,1152]{1,0:T(8,128)(2,1)S(1)}, u32[]{:S(2)}, u32[]{:S(2)}) collective-permute-start(bf16[192,1152]{1,0:T(8,128)(2,1)S(1)} %take_half.1.refs_0_), channel_id=1, source_target_pairs={{8,16},{12,20},{16,8},{20,12},{9,17},{13,21},{17,9},{21,13},{10,18... | collective-permute-start | bytes 1327112 | tf_op jit(solution)/shard_map/mid/ppermute | solution.py:422
  16.6 15.4 %collective-permute-start.4 = (bf16[192,1152]{1,0:T(8,128)(2,1)S(1)}, bf16[192,1152]{1,0:T(8,128)(2,1)S(1)}, u32[]{:S(2)}, u32[]{:S(2)}) collective-permute-start(bf16[192,1152]{1,0:T(8,128)(2,1)S(1)} %collective-permute-done.2.between_ref), channel_id=1, source_target_pairs={{8,0},{12,4},{16,24},{20,28},{9,1},{13,5},{17,25},{21,29},{10,2},{... | collective-permute-start | bytes 1327112 | tf_op jit(solution)/shard_map/end_mid/ppermute | solution.py:422
  17.9 14.4 %collective-permute-start.3 = (bf16[192,1152]{1,0:T(8,128)(2,1)S(1)}, bf16[192,1152]{1,0:T(8,128)(2,1)S(1)}, u32[]{:S(2)}, u32[]{:S(2)}) collective-permute-start(bf16[192,1152]{1,0:T(8,128)(2,1)S(1)} %collective-permute-done.1.refs_2_), channel_id=1, source_target_pairs={{0,4},{4,0},{8,12},{12,8},{16,20},{20,16},{24,28},{28,24},{1,5},{5... | collective-permute-start | bytes 1327112 | tf_op jit(solution)/shard_map/near_across/ppermute | solution.py:428
  18.3 14.6 %collective-permute-start.6 = (bf16[192,1152]{1,0:T(8,128)(2,1)S(1)}, bf16[192,1152]{1,0:T(8,128)(2,1)S(1)}, u32[]{:S(2)}, u32[]{:S(2)}) collective-permute-start(bf16[192,1152]{1,0:T(8,128)(2,1)S(1)} %collective-permute-done.1.refs_2_), channel_id=1, source_target_pairs={{8,16},{12,20},{16,8},{20,12},{9,17},{13,21},{17,9},{21,13},{10,18... | collective-permute-start | bytes 1327112 | tf_op jit(solution)/shard_map/mid_far/ppermute | solution.py:422
  32.3 10.7 %collective-permute-start.5 = (bf16[192,1152]{1,0:T(8,128)(2,1)S(1)}, bf16[192,1152]{1,0:T(8,128)(2,1)S(1)}, u32[]{:S(2)}, u32[]{:S(2)}) collective-permute-start(bf16[192,1152]{1,0:T(8,128)(2,1)S(1)} %choose.2.refs_0_.refs_4_), channel_id=1, source_target_pairs={{0,4},{4,0},{8,12},{12,8},{16,20},{20,16},{24,28},{28,24},{1,5},{5... | collective-permute-start | bytes 1327112 | tf_op jit(solution)/shard_map/second_across/ppermute | solution.py:428
  32.9 12.8 %collective-permute-start.7 = (bf16[192,1152]{1,0:T(8,128)(2,1)S(1)}, bf16[192,1152]{1,0:T(8,128)(2,1)S(1)}, u32[]{:S(2)}, u32[]{:S(2)}) collective-permute-start(bf16[192,1152]{1,0:T(8,128)(2,1)S(1)} %collective-permute-done.6.between_ref), channel_id=1, source_target_pairs={{8,0},{12,4},{16,24},{20,28},{9,1},{13,5},{17,25},{21,29},{10,2},{... | collective-permute-start | bytes 1327112 | tf_op jit(solution)/shard_map/end_far/ppermute | solution.py:422
  34.4 16.2 %collective-permute-start.10 = (bf16[256,1536]{1,0:T(8,128)(2,1)S(1)}, bf16[256,1536]{1,0:T(8,128)(2,1)S(1)}, u32[]{:S(2)}, u32[]{:S(2)}) collective-permute-start(bf16[256,1536]{1,0:T(8,128)(2,1)S(1)} %get-tuple-element.31), channel_id=1, source_target_pairs={{1,3},{5,7},{9,11},{13,15},{17,19},{21,23},{25,27},{29,31}} | collective-permute-start | bytes 2359304 | tf_op jit(solution)/shard_map/halo/ppermute | solution.py:494
  43.1 8.8 %collective-permute-start.11 = (bf16[256,1536]{1,0:T(8,128)(2,1)S(1)}, bf16[256,1536]{1,0:T(8,128)(2,1)S(1)}, u32[]{:S(2)}, u32[]{:S(2)}) collective-permute-start(bf16[256,1536]{1,0:T(8,128)(2,1)S(1)} %get-tuple-element.35), channel_id=1, source_target_pairs={{1,3},{5,7},{9,11},{13,15},{17,19},{21,23},{25,27},{29,31}} | collective-permute-start | bytes 2359304 | tf_op jit(solution)/shard_map/halo/ppermute | solution.py:494
  45.9 10.5 %copy-start.2 = (s32[1,3]{1,0:T(1,128)S(1)}, s32[1,3]{1,0:T(1,128)}, u32[]{:S(2)}) copy-start(s32[1,3]{1,0:T(1,128)} %start_ref.3) | copy-start | bytes 40
  45.9 10.5 %copy-start.3 = (s32[1,12]{1,0:T(1,128)S(1)}, s32[1,12]{1,0:T(1,128)}, u32[]{:S(2)}) copy-start(s32[1,12]{1,0:T(1,128)} %owner_ref.3) | copy-start | bytes 148
  46.0 10.5 %copy-start.4 = (s32[1,12]{1,0:T(1,128)S(1)}, s32[1,12]{1,0:T(1,128)}, u32[]{:S(2)}) copy-start(s32[1,12]{1,0:T(1,128)} %left_ref.3) | copy-start | bytes 148
  46.0 10.4 %collective-permute-start.8 = (bf16[192,1152]{1,0:T(8,128)(2,1)S(1)}, bf16[192,1152]{1,0:T(8,128)(2,1)S(1)}, u32[]{:S(2)}, u32[]{:S(2)}) collective-permute-start(bf16[192,1152]{1,0:T(8,128)(2,1)S(1)} %choose.3.refs_6_), channel_id=1, source_target_pairs={{0,4},{4,0},{8,12},{12,8},{16,20},{20,16},{24,28},{28,24},{1,5},{5... | collective-permute-start | bytes 1327112 | tf_op jit(solution)/shard_map/third_across/ppermute | solution.py:428
  50.6 14.4 %collective-permute-start.12 = (bf16[256,1536]{1,0:T(8,128)(2,1)S(1)}, bf16[256,1536]{1,0:T(8,128)(2,1)S(1)}, u32[]{:S(2)}, u32[]{:S(2)}) collective-permute-start(bf16[256,1536]{1,0:T(8,128)(2,1)S(1)} %collective-permute-done.10.refs_10_), channel_id=1, source_target_pairs={{1,0},{3,2},{5,4},{7,6},{9,8},{11,10},{13,12},{15,14},{17,16},{19,... | collective-permute-start | bytes 2359304 | tf_op jit(solution)/shard_map/halo_first/ppermute | solution.py:500
  51.9 13.1 %collective-permute-start.13 = (bf16[256,1536]{1,0:T(8,128)(2,1)S(1)}, bf16[256,1536]{1,0:T(8,128)(2,1)S(1)}, u32[]{:S(2)}, u32[]{:S(2)}) collective-permute-start(bf16[256,1536]{1,0:T(8,128)(2,1)S(1)} %collective-permute-done.11.refs_11_), channel_id=1, source_target_pairs={{1,0},{3,2},{5,4},{7,6},{9,8},{11,10},{13,12},{15,14},{17,16},{19,... | collective-permute-start | bytes 2359304 | tf_op jit(solution)/shard_map/halo_first/ppermute | solution.py:500
  64.9 3.7 %collective-permute-start.14 = (bf16[1024,384]{1,0:T(8,128)(2,1)S(1)}, bf16[1024,384]{1,0:T(8,128)(2,1)S(1)}, u32[]{:S(2)}, u32[]{:S(2)}) collective-permute-start(bf16[1024,384]{1,0:T(8,128)(2,1)S(1)} %get-tuple-element.44.refs_2_), channel_id=1, source_target_pairs={{0,1},{1,0},{2,3},{3,2},{4,5},{5,4},{6,7},{7,6},{8,9},{9,8},{10,11... | collective-permute-start | bytes 2359304 | tf_op jit(solution)/shard_map/swap/ppermute | solution.py:505
